TPU v7x, 32 devices: a whole 2x2x4 slice. The times are simulated.
32 devices in a mesh: dp: 8 (over y, x, core), tensor: 4 (over z).
Axes of the slice: x: 2, y: 2, z: 4, core: 2. Of those that a mesh axis runs over, the one named last changes fastest.
Arguments:
- tokens: bfloat16 [8192, 2048], P(('dp', 'tensor')), may hold values from -6 to 6
- cotangent: bfloat16 [8192, 2048], P(('dp', 'tensor')), may hold values from -6 to 6
- doc_start: int32 [8192], P('dp'), may hold values from 0 to 1023, as said below
- in_weight: float32 [2048, 3, 2048], P('dp', None, 'tensor'), may hold values from -0.125 to 0.125
- in_first: float32 [2048, 3, 2048], P('dp', None, 'tensor'), may hold values from -32 to 32
- in_second: float32 [2048, 3, 2048], P('dp', None, 'tensor'), may hold values from 106.496 to 434.176
- out_weight: float32 [2048, 2048], P('tensor', 'dp'), may hold values from -0.375 to 0.375
- out_first: float32 [2048, 2048], P('tensor', 'dp'), may hold values from -16 to 16
- out_second: float32 [2048, 2048], P('tensor', 'dp'), may hold values from 27.0336 to 106.496
- gate_up: float32 [2048, 2, 8192], P('dp', None, 'tensor'), may hold values from -0.125 to 0.125
- gate_up_first: float32 [2048, 2, 8192], P('dp', None, 'tensor'), may hold values from -16 to 16
- gate_up_second: float32 [2048, 2, 8192], P('dp', None, 'tensor'), may hold values from 38.5024 to 155.648
- down_weight: float32 [8192, 2048], P('tensor', 'dp'), may hold values from -0.0625 to 0.0625
- down_first: float32 [8192, 2048], P('tensor', 'dp'), may hold values from -32 to 32
- down_second: float32 [8192, 2048], P('tensor', 'dp'), may hold values from 155.648 to 622.592
- norm_gains: float32 [2, 2048], P(None, 'dp'), may hold values from 0.5 to 1.5
- gains_first: float32 [2, 2048], P(None, 'dp'), may hold values from -56 to 56
- gains_second: float32 [2, 2048], P(None, 'dp'), may hold values from 352.256 to 1392.64
Outputs:
- output: bfloat16 [8192, 2048], P(('dp', 'tensor'))
- input_grad: float32 [8192, 2048], P(('dp', 'tensor'))
- new_in_first: float32 [2048, 3, 2048], P('dp', None, 'tensor')
- new_in_second: float32 [2048, 3, 2048], P('dp', None, 'tensor')
- new_in_weight: float32 [2048, 3, 2048], P('dp', None, 'tensor')
- new_out_first: float32 [2048, 2048], P('tensor', 'dp')
- new_out_second: float32 [2048, 2048], P('tensor', 'dp')
- new_out_weight: float32 [2048, 2048], P('tensor', 'dp')
- new_gate_up_first: float32 [2048, 2, 8192], P('dp', None, 'tensor')
- new_gate_up_second: float32 [2048, 2, 8192], P('dp', None, 'tensor')
- new_gate_up: float32 [2048, 2, 8192], P('dp', None, 'tensor')
- new_down_first: float32 [8192, 2048], P('tensor', 'dp')
- new_down_second: float32 [8192, 2048], P('tensor', 'dp')
- new_down_weight: float32 [8192, 2048], P('tensor', 'dp')
- new_gains_first: float32 [2, 2048], P(None, 'dp')
- new_gains_second: float32 [2, 2048], P(None, 'dp')
- new_norm_gains: float32 [2, 2048], P(None, 'dp')
Inputs may be any that keep to these rules, and one draw needn't show every extreme that they name: doc_start[t] is the slot, counted from 0 within t's data group of 1024 consecutive tokens, of the first token of t's document: within a group values never fall and each equals the slot at which it first appears, so documents are runs of equal values; one data group holds a single document of 1024 tokens.
All inputs are finite; a program needn't handle non-finite values.
Results may differ from a plain program's by a relative error of at most 0.028.
Values may be sent and summed in bfloat16 or wider, within the bound.
A program may use at most 320 MiB of HBM per device.

v0:
```python
import jax
import jax.numpy as jnp
from jax import lax
from jax.sharding import PartitionSpec as P

D = 2048
HEAD_DIM = 64
FF = 8192
STEP = 5


EPSILON = 1e-05
ROPE_BASE = 130000.0
BETA_ONE = 0.9
BETA_TWO = 0.95
ADAM_EPSILON = 1e-08
WEIGHT_DECAY = 0.1
GAIN_RATE = 0.5
MASK_VALUE = -1e30


def rotary_tables(starts):
    places = (jnp.arange(starts.shape[0], dtype=jnp.int32) - starts).astype(jnp.float32)
    powers = jnp.arange(HEAD_DIM // 2, dtype=jnp.float32) * (2.0 / HEAD_DIM)
    angles = places[:, None] * (ROPE_BASE ** (-powers))[None, :]
    return (jnp.cos(angles)[:, None, :], jnp.sin(angles)[:, None, :])


def rotate(tensor, cosine, sine):
    half = tensor.shape[-1] // 2
    lower = tensor[..., :half]
    upper = tensor[..., half:]
    return jnp.concatenate([lower * cosine - upper * sine, upper * cosine + lower * sine], axis=-1)


def unrotate(tensor, cosine, sine):
    half = tensor.shape[-1] // 2
    lower = tensor[..., :half]
    upper = tensor[..., half:]
    return jnp.concatenate([lower * cosine + upper * sine, upper * cosine - lower * sine], axis=-1)


def block_scores(query_rows, key_rows, starts, start_row, stop_row):
    raw = jnp.einsum("qhd,khd->hqk", query_rows, key_rows, preferred_element_type=jnp.float32)
    query_index = jnp.arange(start_row, stop_row, dtype=jnp.int32)
    key_index = jnp.arange(stop_row, dtype=jnp.int32)
    allowed = (starts[start_row:stop_row][:, None] == starts[:stop_row][None, :]) & (
        key_index[None, :] <= query_index[:, None]
    )
    return jnp.where(allowed[None], raw * HEAD_DIM ** (-0.5), MASK_VALUE)


def norm_back(grad_normed, gain, normed, scale):
    scaled = grad_normed * gain
    return scale * (scaled - normed * jnp.mean(scaled * normed, axis=-1, keepdims=True))


def adam_step(weight, first_moment, second_moment, grad, rate, decay):
    new_first = BETA_ONE * first_moment + (1.0 - BETA_ONE) * grad
    new_second = BETA_TWO * second_moment + (1.0 - BETA_TWO) * grad * grad
    mean_part = new_first / (1.0 - BETA_ONE**STEP)
    size_part = jnp.sqrt(new_second / (1.0 - BETA_TWO**STEP)) + ADAM_EPSILON
    new_weight = weight - rate * (mean_part / size_part + decay * weight)
    return (new_first, new_second, new_weight)


def local(
    tokens,
    cotangent,
    doc_start,
    in_weight,
    in_first,
    in_second,
    out_weight,
    out_first,
    out_second,
    gate_up,
    gate_up_first,
    gate_up_second,
    down_weight,
    down_first,
    down_second,
    norm_gains,
    gains_first,
    gains_second,
):
    half_type = jnp.bfloat16
    full_type = jnp.float32
    in_w, out_w, up_w, down_w, gain_w = (
        lax.all_gather(in_weight.astype(half_type), "dp", axis=0, tiled=True),
        lax.all_gather(out_weight.astype(half_type), "dp", axis=1, tiled=True),
        lax.all_gather(gate_up.astype(half_type), "dp", axis=0, tiled=True),
        lax.all_gather(down_weight.astype(half_type), "dp", axis=1, tiled=True),
        lax.all_gather(norm_gains.astype(half_type), "dp", axis=1, tiled=True),
    )
    width = in_w.shape[0]
    local_width = in_w.shape[2]
    local_hidden = up_w.shape[2]
    local_heads = local_width // HEAD_DIM
    count = doc_start.shape[0]
    in_matrix = in_w.reshape(width, 3 * local_width)
    up_matrix = up_w.reshape(width, 2 * local_hidden)
    gain_one = gain_w[0].astype(full_type)
    gain_two = gain_w[1].astype(full_type)
    resid = tokens.astype(full_type)
    scale_one = lax.rsqrt(jnp.mean(resid * resid, axis=-1, keepdims=True) + EPSILON)
    normed_one = resid * scale_one
    h_one = (normed_one * gain_one).astype(half_type)
    rows_one, back_rows = (
        lax.all_gather(h_one, "tensor", axis=0, tiled=True),
        lax.all_gather(cotangent, "tensor", axis=0, tiled=True),
    )
    cosine, sine = rotary_tables(doc_start)
    projected = jnp.dot(rows_one, in_matrix, preferred_element_type=full_type).reshape(
        count, 3, local_heads, HEAD_DIM
    )
    query = rotate(projected[:, 0], cosine, sine).astype(half_type)
    keys = rotate(projected[:, 1], cosine, sine).astype(half_type)
    values = projected[:, 2].astype(half_type)
    block_rows = min(512, count)
    block_outputs = []
    block_totals = []
    for start_row in range(0, count, block_rows):
        stop_row = start_row + block_rows
        scores = block_scores(
            query[start_row:stop_row], keys[:stop_row], doc_start, start_row, stop_row
        )
        peak = jnp.max(scores, axis=-1, keepdims=True)
        expo = jnp.exp(scores - peak)
        total = jnp.sum(expo, axis=-1, keepdims=True)
        probs_low = (expo / total).astype(half_type)
        block_outputs.append(
            jnp.einsum(
                "hqk,khd->qhd", probs_low, values[:stop_row], preferred_element_type=full_type
            )
        )
        block_totals.append(peak + jnp.log(total))
    attended = jnp.concatenate(block_outputs, axis=0).reshape(count, local_width).astype(half_type)
    branch = lax.psum_scatter(
        jnp.dot(attended, out_w, preferred_element_type=full_type).astype(jnp.bfloat16),
        "tensor",
        scatter_dimension=0,
        tiled=True,
    ).astype(jnp.float32)
    hidden_in = resid + branch
    scale_two = lax.rsqrt(jnp.mean(hidden_in * hidden_in, axis=-1, keepdims=True) + EPSILON)
    normed_two = hidden_in * scale_two
    h_two = (normed_two * gain_two).astype(half_type)
    rows_two = lax.all_gather(h_two, "tensor", axis=0, tiled=True)
    both = jnp.dot(rows_two, up_matrix, preferred_element_type=full_type).reshape(
        count, 2, local_hidden
    )
    gate_part = both[:, 0]
    up_part = both[:, 1]
    sigmoid_gate = jax.nn.sigmoid(gate_part)
    silu_gate = gate_part * sigmoid_gate
    inner = (silu_gate * up_part).astype(half_type)
    mlp_out = lax.psum_scatter(
        jnp.dot(inner, down_w, preferred_element_type=full_type).astype(jnp.bfloat16),
        "tensor",
        scatter_dimension=0,
        tiled=True,
    ).astype(jnp.float32)
    output = (hidden_in + mlp_out).astype(half_type)
    down_grad = jnp.dot(inner.T, back_rows, preferred_element_type=full_type)
    d_inner = jnp.dot(back_rows, down_w.T, preferred_element_type=full_type)
    d_gate = d_inner * up_part * sigmoid_gate * (1.0 + gate_part * (1.0 - sigmoid_gate))
    d_up = d_inner * silu_gate
    d_both = jnp.stack([d_gate, d_up], axis=1).astype(half_type).reshape(count, 2 * local_hidden)
    up_grad = jnp.dot(rows_two.T, d_both, preferred_element_type=full_type).reshape(
        width, 2, local_hidden
    )
    d_two = lax.psum_scatter(
        jnp.dot(d_both, up_matrix.T, preferred_element_type=full_type).astype(jnp.bfloat16),
        "tensor",
        scatter_dimension=0,
        tiled=True,
    ).astype(jnp.float32)
    d_hidden = cotangent.astype(full_type) + norm_back(d_two, gain_two, normed_two, scale_two)
    gain_two_part = jnp.sum(d_two * normed_two, axis=0)
    branch_back = lax.all_gather(d_hidden.astype(half_type), "tensor", axis=0, tiled=True)
    out_grad = jnp.dot(attended.T, branch_back, preferred_element_type=full_type)
    d_attended = (
        jnp.dot(branch_back, out_w.T, preferred_element_type=full_type)
        .astype(half_type)
        .reshape(count, local_heads, HEAD_DIM)
    )
    query_grads = []
    key_grad = jnp.zeros((count, local_heads, HEAD_DIM), full_type)
    value_grad = jnp.zeros((count, local_heads, HEAD_DIM), full_type)
    for block_number, start_row in enumerate(range(0, count, block_rows)):
        stop_row = start_row + block_rows
        scores = block_scores(
            query[start_row:stop_row], keys[:stop_row], doc_start, start_row, stop_row
        )
        probs = jnp.exp(scores - block_totals[block_number])
        d_probs = jnp.einsum(
            "qhd,khd->hqk",
            d_attended[start_row:stop_row],
            values[:stop_row],
            preferred_element_type=full_type,
        )
        centre = jnp.sum(probs * d_probs, axis=-1, keepdims=True)
        d_scores = (probs * (d_probs - centre) * HEAD_DIM ** (-0.5)).astype(half_type)
        query_grads.append(
            jnp.einsum("hqk,khd->qhd", d_scores, keys[:stop_row], preferred_element_type=full_type)
        )
        key_grad = key_grad.at[:stop_row].add(
            jnp.einsum(
                "hqk,qhd->khd",
                d_scores,
                query[start_row:stop_row],
                preferred_element_type=full_type,
            )
        )
        value_grad = value_grad.at[:stop_row].add(
            jnp.einsum(
                "hqk,qhd->khd",
                probs.astype(half_type),
                d_attended[start_row:stop_row],
                preferred_element_type=full_type,
            )
        )
    query_grad = jnp.concatenate(query_grads, axis=0)
    d_projected = jnp.stack(
        [unrotate(query_grad, cosine, sine), unrotate(key_grad, cosine, sine), value_grad], axis=1
    )
    d_projected = d_projected.astype(half_type).reshape(count, 3 * local_width)
    in_grad = jnp.dot(rows_one.T, d_projected, preferred_element_type=full_type).reshape(
        width, 3, local_width
    )
    d_one = lax.psum_scatter(
        jnp.dot(d_projected, in_matrix.T, preferred_element_type=full_type).astype(jnp.bfloat16),
        "tensor",
        scatter_dimension=0,
        tiled=True,
    ).astype(jnp.float32)
    input_grad = d_hidden + norm_back(d_one, gain_one, normed_one, scale_one)
    gain_one_part = jnp.sum(d_one * normed_one, axis=0)
    gain_total = lax.psum(jnp.stack([gain_one_part, gain_two_part]), "tensor")
    in_summed, out_summed, up_summed, down_summed, gain_summed = (
        lax.psum_scatter(
            in_grad.astype(jnp.bfloat16), "dp", scatter_dimension=0, tiled=True
        ).astype(jnp.float32),
        lax.psum_scatter(
            out_grad.astype(jnp.bfloat16), "dp", scatter_dimension=1, tiled=True
        ).astype(jnp.float32),
        lax.psum_scatter(
            up_grad.astype(jnp.bfloat16), "dp", scatter_dimension=0, tiled=True
        ).astype(jnp.float32),
        lax.psum_scatter(
            down_grad.astype(jnp.bfloat16), "dp", scatter_dimension=1, tiled=True
        ).astype(jnp.float32),
        lax.psum_scatter(
            gain_total.astype(jnp.bfloat16), "dp", scatter_dimension=1, tiled=True
        ).astype(jnp.float32),
    )
    in_new = adam_step(in_weight, in_first, in_second, in_summed, 2.0 * D ** (-0.5), WEIGHT_DECAY)
    out_new = adam_step(
        out_weight, out_first, out_second, out_summed, 2.0 * (D // 8) ** (-0.5), WEIGHT_DECAY
    )
    up_new = adam_step(
        gate_up, gate_up_first, gate_up_second, up_summed, 2.0 * D ** (-0.5), WEIGHT_DECAY
    )
    down_new = adam_step(
        down_weight, down_first, down_second, down_summed, 2.0 * FF ** (-0.5), WEIGHT_DECAY
    )
    gain_new = adam_step(norm_gains, gains_first, gains_second, gain_summed, GAIN_RATE, 0.0)
    return (
        output,
        input_grad,
        in_new[0],
        in_new[1],
        in_new[2],
        out_new[0],
        out_new[1],
        out_new[2],
        up_new[0],
        up_new[1],
        up_new[2],
        down_new[0],
        down_new[1],
        down_new[2],
        gain_new[0],
        gain_new[1],
        gain_new[2],
    )


def solution(mesh):
    in_specs = (
        P(("dp", "tensor"), None),
        P(("dp", "tensor"), None),
        P("dp"),
        P("dp", None, "tensor"),
        P("dp", None, "tensor"),
        P("dp", None, "tensor"),
        P("tensor", "dp"),
        P("tensor", "dp"),
        P("tensor", "dp"),
        P("dp", None, "tensor"),
        P("dp", None, "tensor"),
        P("dp", None, "tensor"),
        P("tensor", "dp"),
        P("tensor", "dp"),
        P("tensor", "dp"),
        P(None, "dp"),
        P(None, "dp"),
        P(None, "dp"),
    )
    out_specs = (
        P(("dp", "tensor"), None),
        P(("dp", "tensor"), None),
        P("dp", None, "tensor"),
        P("dp", None, "tensor"),
        P("dp", None, "tensor"),
        P("tensor", "dp"),
        P("tensor", "dp"),
        P("tensor", "dp"),
        P("dp", None, "tensor"),
        P("dp", None, "tensor"),
        P("dp", None, "tensor"),
        P("tensor", "dp"),
        P("tensor", "dp"),
        P("tensor", "dp"),
        P(None, "dp"),
        P(None, "dp"),
        P(None, "dp"),
    )
    return jax.shard_map(local, mesh=mesh, in_specs=in_specs, out_specs=out_specs, check_vma=False)
```

profile of v0, /device:TPU:8, one launch (start us, length us, event | category | flops | bytes accessed | tf_op | source)
XLA Modules:
  0.0 1476.5 jit_solution(18145990281309441940)
XLA Ops:
  25.4 74.2 %all-gather.9.cloned.1.call-done = bf16[1024,2048]{1,0:T(8,128)(2,1)} async-done(((bf16[256,2048]{1,0:T(8,128)(2,1)}), bf16[1024,2048]{1,0:T(8,128)(2,1)}) %all-gather.9.cloned.1.call-update) | async-done | bytes 4194320 | tf_op jit(solution)/shard_map/all_gather | solution.py:110
  99.6 50.3 %all-gather.11.cloned.1.call-done = bf16[2048,3,512]{0,2,1:T(8,128)(2,1)} async-done(((bf16[256,3,512]{0,2,1:T(8,128)(2,1)}), bf16[2048,3,512]{0,2,1:T(8,128)(2,1)}) %all-gather.11.cloned.1.call-update) | async-done | bytes 6291472 | tf_op jit(solution)/shard_map/all_gather | solution.py:90
  194.0 71.0 %reduce-scatter.12.cloned.1.call-done = bf16[256,2048]{1,0:T(8,128)(2,1)} async-done(((bf16[1024,2048]{1,0:T(8,128)(2,1)}), bf16[256,2048]{1,0:T(8,128)(2,1)}) %reduce-scatter.12.cloned.1.call-update) | async-done | bytes 1048592 | tf_op jit(solution)/shard_map/reduce_scatter | solution.py:139
  270.1 87.8 %all-gather.17.cloned.1.call-done = bf16[2048,2,2048]{2,0,1:T(8,128)(2,1)} async-done(((bf16[256,2,2048]{2,0,1:T(8,128)(2,1)}), bf16[2048,2,2048]{2,0,1:T(8,128)(2,1)}) %all-gather.17.cloned.1.call-update) | async-done | bytes 16777232 | tf_op jit(solution)/shard_map/all_gather | solution.py:92
  357.9 23.0 %copy.69 = bf16[2048,2,2048]{0,2,1:T(8,128)(2,1)} copy(bf16[2048,2,2048]{2,0,1:T(8,128)(2,1)} %all-gather.17.cloned.1.call-done) | data formatting | bytes 33554432 | tf_op jit(solution)/shard_map/all_gather | solution.py:92
  380.9 57.3 %all-gather.15.cloned.1.call-done = bf16[1024,2048]{1,0:T(8,128)(2,1)} async-done(((bf16[256,2048]{1,0:T(8,128)(2,1)}), bf16[1024,2048]{1,0:T(8,128)(2,1)}) %all-gather.15.cloned.1.call-update) | async-done | bytes 4194320 | tf_op jit(solution)/shard_map/all_gather | solution.py:149
  438.1 21.6 %fusion.2 = f32[1024,2,2048]{2,0,1:T(8,128)S(1)} fusion(bf16[2048,2,2048]{0,2,1:T(8,128)(2,1)} %copy.69, bf16[1024,2048]{1,0:T(8,128)(2,1)} %all-gather.15.cloned.1.call-done), kind=kOutput, calls=%fused_computation.3 | convolution fusion | flops 17179869184 | bytes 37748736 | tf_op jit(solution)/shard_map/dot_general | solution.py:150
  469.3 49.8 %all-gather.21.cloned.1.call-done = bf16[1024,2048]{1,0:T(8,128)(2,1)} async-done(((bf16[256,2048]{1,0:T(8,128)(2,1)}), bf16[1024,2048]{1,0:T(8,128)(2,1)}) %all-gather.21.cloned.1.call-update) | async-done | bytes 4194320 | tf_op jit(solution)/shard_map/all_gather | solution.py:111
  533.2 72.6 %reduce-scatter.26.cloned.1.call-done = bf16[2048,256]{1,0:T(8,128)(2,1)} async-done(((bf16[2048,2048]{1,0:T(8,128)(2,1)}), bf16[2048,256]{1,0:T(8,128)(2,1)}) %reduce-scatter.26.cloned.1.call-update) | async-done | bytes 1048592 | tf_op jit(solution)/shard_map/reduce_scatter | solution.py:251
  612.5 56.1 %all-gather.19.cloned.1.call-done = bf16[2048,2048]{1,0:T(8,128)(2,1)} async-done(((bf16[2048,256]{1,0:T(8,128)(2,1)}), bf16[2048,2048]{1,0:T(8,128)(2,1)}) %all-gather.19.cloned.1.call-update) | async-done | bytes 8388624 | tf_op jit(solution)/shard_map/all_gather | solution.py:93
  668.6 19.9 %multiply_bitcast_fusion.1 = (bf16[1024,1,2048]{2,0,1:T(8,128)(2,1)S(1)}, bf16[1024,1,2048]{2,0,1:T(8,128)(2,1)}) fusion(f32[1024,2,2048]{2,0,1:T(8,128)} %copy-done.6, bf16[1024,2048]{1,0:T(8,128)(2,1)} %all-gather.21.cloned.1.call-done, bf16[2048,2048]{1,0:T(8,128)(2,1)} %all-gather.19.cloned.1.call-done), kind=kOutput, calls=%fused_computation.30 | convolution fusion | flops 8617197568 | bytes 37748736 | tf_op jit(solution)/shard_map/dot_general | solution.py:166
  690.6 22.8 %bitcast_convert_fusion = bf16[1024,2048]{1,0:T(8,128)(2,1)} fusion(bf16[2048,2,2048]{2,0,1:T(8,128)(2,1)} %all-gather.17.cloned.1.call-done, bf16[1024,1,2048]{2,0,1:T(8,128)(2,1)} %get-tuple-element.152, bf16[1024,1,2048]{2,0,1:T(8,128)(2,1)S(1)} %get-tuple-element.151), kind=kOutput, calls=%fused_computation.21 | convolution fusion | flops 17186160640 | bytes 29360128 | tf_op jit(solution)/shard_map/dot_general | solution.py:174
  713.5 76.8 %reduce-scatter.16.cloned.1.call-done = bf16[256,2048]{1,0:T(8,128)(2,1)} async-done(((bf16[1024,2048]{1,0:T(8,128)(2,1)}), bf16[256,2048]{1,0:T(8,128)(2,1)}) %reduce-scatter.16.cloned.1.call-update) | async-done | bytes 1048592 | tf_op jit(solution)/shard_map/reduce_scatter | solution.py:173
  795.9 78.7 %all-gather.23.cloned.1.call-done = bf16[1024,2048]{1,0:T(8,128)(2,1)} async-done(((bf16[256,2048]{1,0:T(8,128)(2,1)}), bf16[1024,2048]{1,0:T(8,128)(2,1)}) %all-gather.23.cloned.1.call-update) | async-done | bytes 4194320 | tf_op jit(solution)/shard_map/all_gather | solution.py:181
  892.2 14.7 fusion.100
  939.3 29.9 %fusion.97 = f32[512,8,64]{0,2,1:T(8,128)} fusion(f32[8,512,1024]{2,1,0:T(8,128)} %fusion.112, f32[8,512,1024]{2,1,0:T(8,128)} %copy-done, f32[8,512]{1,0:T(8,128)S(1)} %log_add_fusion, bf16[1024,8,32]{0,2,1:T(8,128)(2,1)S(1)} %copy-done.15, bf16[1024,8,32]{0,2,1:T(8,128)(2,1)} %copy-done.16), kind=kOutput, calls=%fused_computation.126 | convolution fusion | flops 568333312 | bytes 35667968 | tf_op jit(solution)/shard_map/hqk,khd->qhd/dot_general | solution.py:206
  969.2 30.9 %bitcast_add_fusion.1 = f32[1024,8,64]{0,2,1:T(8,128)} fusion(f32[512,8,64]{0,2,1:T(8,128)} %fusion.103, f32[8,512,1024]{2,1,0:T(8,128)} %fusion.112, f32[8,512,1024]{2,1,0:T(8,128)} %copy-done, f32[8,512]{1,0:T(8,128)S(1)} %log_add_fusion, bf16[1024,8,32]{0,2,1:T(8,128)(2,1)S(1)} %copy-done.13, bf16[1024,8,32]{0,2,1:T(8,128)(2,1)S(1)} %copy-done.11), kind=kOutput, calls=%fused_computation.112 | convolution fusion | flops 567809024 | bytes 37765120 | tf_op jit(solution)/shard_map/hqk,qhd->khd/dot_general | solution.py:209
  1036.2 56.4 %reduce-scatter.18.cloned.1.call-done = bf16[256,2048]{1,0:T(8,128)(2,1)} async-done(((bf16[1024,2048]{1,0:T(8,128)(2,1)}), bf16[256,2048]{1,0:T(8,128)(2,1)}) %reduce-scatter.18.cloned.1.call-update) | async-done | bytes 1048592 | tf_op jit(solution)/shard_map/reduce_scatter | solution.py:232
  1094.7 14.7 psum.7
  1142.1 24.8 %convolution_convert_fusion = bf16[2048,2,2048]{2,0,1:T(8,128)(2,1)} fusion(bf16[1024,2,2048]{0,2,1:T(8,128)(2,1)} %copy.75, bf16[1024,2048]{1,0:T(8,128)(2,1)} %all-gather.15.cloned.1.call-done), kind=kOutput, calls=%fused_computation.14 | convolution fusion | flops 17188257792 | bytes 29360128 | tf_op jit(solution)/shard_map/dot_general | solution.py:170
  1170.0 47.2 %reduce-scatter.14.cloned.1.call-done = bf16[256,2048]{1,0:T(8,128)(2,1)} async-done(((bf16[1024,2048]{1,0:T(8,128)(2,1)}), bf16[256,2048]{1,0:T(8,128)(2,1)}) %reduce-scatter.14.cloned.1.call-update) | async-done | bytes 1048592 | tf_op jit(solution)/shard_map/reduce_scatter | solution.py:158
  1222.5 32.9 %reduce-scatter.28.cloned.1.call-done = bf16[256,2]{1,0:T(8,128)(2,1)} async-done(((bf16[2048,2]{1,0:T(8,128)(2,1)}), bf16[256,2]{1,0:T(8,128)(2,1)}) %reduce-scatter.28.cloned.1.call-update) | async-done | bytes 1040
  1257.0 63.8 %reduce-scatter.20.cloned.1.call-done = bf16[256,3,512]{2,0,1:T(8,128)(2,1)} async-done(((bf16[2048,3,512]{2,0,1:T(8,128)(2,1)}), bf16[256,3,512]{2,0,1:T(8,128)(2,1)}) %reduce-scatter.20.cloned.1.call-update) | async-done | bytes 786448 | tf_op jit(solution)/shard_map/reduce_scatter | solution.py:242
  1326.5 113.7 %reduce-scatter.24.cloned.1.call-done = bf16[256,2,2048]{2,0,1:T(8,128)(2,1)} async-done(((bf16[2048,2,2048]{2,0,1:T(8,128)(2,1)}), bf16[256,2,2048]{2,0,1:T(8,128)(2,1)}) %reduce-scatter.24.cloned.1.call-update) | async-done | bytes 2097168 | tf_op jit(solution)/shard_map/reduce_scatter | solution.py:248
  (222 shorter events, 270.5 us)
Async XLA Ops:
  7.2 92.4 %all-gather.9.cloned.1.call-start = ((), (), s32[]{:S(2)}) async-start(), calls=%async_computation.9 | async-start | bytes 5242880 | tf_op jit(solution)/shard_map/all_gather | solution.py:110
  18.6 248.1 %copy-start.33 = (f32[1,2048]{1,0:T(1,128)}, f32[1,2048]{1,0:T(1,128)S(1)}, u32[]{:S(2)}) copy-start(f32[1,2048]{1,0:T(1,128)S(1)} %get-tuple-element.172) | copy-start | bytes 24580
  21.1 128.8 %all-gather.11.cloned.1.call-start = ((), (), s32[]{:S(2)}) async-start(), calls=%async_computation.10 | async-start | bytes 7077888 | tf_op jit(solution)/shard_map/all_gather | solution.py:90
  22.3 159.4 %all-gather.13.cloned.1.call-start = ((), (), s32[]{:S(2)}) async-start(), calls=%async_computation.11 | async-start | bytes 2359296 | tf_op jit(solution)/shard_map/all_gather | solution.py:91
  23.1 241.9 %reduce-scatter.12.cloned.1.call-start = ((), (), s32[]{:S(2)}) async-start(), calls=%async_computation.12 | async-start | bytes 5242880 | tf_op jit(solution)/shard_map/reduce_scatter | solution.py:139
  23.5 149.0 %copy-start.20 = (pred[512,512]{0,1:T(8,128)(4,1)}, pred[512,512]{0,1:T(8,128)(4,1)S(1)}, u32[]{:S(2)}) copy-start(pred[512,512]{0,1:T(8,128)(4,1)S(1)} %fusion.111) | copy-start | bytes 786436
  24.0 137.6 %copy-start.25 = (f32[1024,32]{0,1:T(8,128)}, f32[1024,32]{0,1:T(8,128)S(1)}, u32[]{:S(2)}) copy-start(f32[1024,32]{0,1:T(8,128)S(1)} %get-tuple-element.174) | copy-start | bytes 393220
  24.0 137.6 %copy-start.27 = (f32[1024,32]{0,1:T(8,128)}, f32[1024,32]{0,1:T(8,128)S(1)}, u32[]{:S(2)}) copy-start(f32[1024,32]{0,1:T(8,128)S(1)} %get-tuple-element.175) | copy-start | bytes 393220
  188.1 169.8 %all-gather.17.cloned.1.call-start = ((), (), s32[]{:S(2)}) async-start(), calls=%async_computation.14 | async-start | bytes 18874368 | tf_op jit(solution)/shard_map/all_gather | solution.py:92
  194.0 244.1 %all-gather.15.cloned.1.call-start = ((), (), s32[]{:S(2)}) async-start(), calls=%async_computation.13 | async-start | bytes 5242880 | tf_op jit(solution)/shard_map/all_gather | solution.py:149
  266.7 114.2 %copy-start.47 = (f32[256]{0:T(256)}, f32[256]{0:T(256)S(1)}, u32[]{:S(2)}) copy-start(f32[256]{0:T(256)S(1)} %add_rsqrt_fusion) | copy-start | bytes 3076
  269.3 249.8 %all-gather.21.cloned.1.call-start = ((), (), s32[]{:S(2)}) async-start(), calls=%async_computation.17 | async-start | bytes 5242880 | tf_op jit(solution)/shard_map/all_gather | solution.py:111
  270.0 335.8 %reduce-scatter.26.cloned.1.call-start = ((), (), s32[]{:S(2)}) async-start(), calls=%async_computation.24 | async-start | bytes 9437184 | tf_op jit(solution)/shard_map/reduce_scatter | solution.py:251
  533.2 135.4 %all-gather.19.cloned.1.call-start = ((), (), s32[]{:S(2)}) async-start(), calls=%async_computation.15 | async-start | bytes 9437184 | tf_op jit(solution)/shard_map/all_gather | solution.py:93
  612.5 177.9 %reduce-scatter.16.cloned.1.call-start = ((), (), s32[]{:S(2)}) async-start(), calls=%async_computation.18 | async-start | bytes 5242880 | tf_op jit(solution)/shard_map/reduce_scatter | solution.py:173
  713.5 161.1 %all-gather.23.cloned.1.call-start = ((), (), s32[]{:S(2)}) async-start(), calls=%async_computation.19 | async-start | bytes 5242880 | tf_op jit(solution)/shard_map/all_gather | solution.py:181
  792.5 87.3 %copy-start.52 = (f32[256]{0:T(256)}, f32[256]{0:T(256)S(1)}, u32[]{:S(2)}) copy-start(f32[256]{0:T(256)S(1)} %broadcast_multiply_fusion.1) | copy-start | bytes 3076
  795.8 296.8 %reduce-scatter.18.cloned.1.call-start = ((), (), s32[]{:S(2)}) async-start(), calls=%async_computation.20 | async-start | bytes 5242880 | tf_op jit(solution)/shard_map/reduce_scatter | solution.py:232
  1014.5 152.6 %reduce-scatter.22.cloned.1.call-start = ((), (), s32[]{:S(2)}) async-start(), calls=%async_computation.22 | async-start | bytes 2359296 | tf_op jit(solution)/shard_map/reduce_scatter | solution.py:245
  1021.6 195.7 %reduce-scatter.14.cloned.1.call-start = ((), (), s32[]{:S(2)}) async-start(), calls=%async_computation.16 | async-start | bytes 5242880 | tf_op jit(solution)/shard_map/reduce_scatter | solution.py:158
  1036.2 219.2 %reduce-scatter.28.cloned.1.call-start = ((), (), s32[]{:S(2)}) async-start(), calls=%async_computation.25 | async-start | bytes 589824
  1110.5 210.3 %reduce-scatter.20.cloned.1.call-start = ((), (), s32[]{:S(2)}) async-start(), calls=%async_computation.21 | async-start | bytes 7077888 | tf_op jit(solution)/shard_map/reduce_scatter | solution.py:242
  1122.2 318.0 %reduce-scatter.24.cloned.1.call-start = ((), (), s32[]{:S(2)}) async-start(), calls=%async_computation.23 | async-start | bytes 18874368 | tf_op jit(solution)/shard_map/reduce_scatter | solution.py:248
  1170.0 86.3 %copy-start.56 = (f32[2,256]{1,0:T(2,128)S(1)}, f32[2,256]{1,0:T(2,128)}, u32[]{:S(2)}) copy-start(f32[2,256]{1,0:T(2,128)} %param.46) | copy-start | bytes 6148
  (52 other events, 1669.0 us)
Sparse Core Ops, SparseCore 0:
  21.2 78.3 all-gather.8
  102.0 47.8 all-gather.10
  152.4 28.1 all-gather.12
  188.2 76.7 reduce-scatter.11
  267.5 90.3 all-gather.16
  360.0 78.1 all-gather.14
  439.8 79.2 all-gather.20
  533.3 72.4 reduce-scatter.25
  612.6 55.9 all-gather.18
  713.6 76.7 reduce-scatter.15
  795.9 78.6 all-gather.22
  1014.6 77.9 reduce-scatter.17
  1096.4 41.7 reduce-scatter.21
  1140.5 76.7 reduce-scatter.13
  1220.8 34.6 reduce-scatter.27
  1259.0 61.7 reduce-scatter.19
  1324.2 115.9 reduce-scatter.23
where the time goes:
time: 1480 us
  waiting for transfers between devices  990 us (67%)
  matrix products  301 us (20%)
  other arithmetic  75.7 us (5%)
  local copies, waits for them, and re-layouts  71.2 us (5%)
  blocking collectives  23.6 us (2%)
  between operations  15 us (1%)
    reduce_scatter x1, waiting for transfers between devices, local(): lax.psum_scatter(up_grad.astype(jnp.bfloat16), 'dp', scatter_dimension=0,...  114 us
    all_gather x1, waiting for transfers between devices, local(): lax.all_gather(gate_up.astype(half_type), 'dp', axis=0, tiled=True)  87.8 us
    all_gather x1, waiting for transfers between devices, local(): lax.all_gather(d_hidden.astype(half_type), 'tensor', axis=0, tiled=True)  78.7 us
    reduce_scatter x1, waiting for transfers between devices, local(): lax.psum_scatter(jnp.dot(d_both, up_matrix.T, preferred_element_type=full...  76.8 us
    all_gather x1, waiting for transfers between devices, local(): lax.all_gather(h_one, 'tensor', axis=0, tiled=True)  74.2 us
    reduce_scatter x1, waiting for transfers between devices, local(): lax.psum_scatter(down_grad.astype(jnp.bfloat16), 'dp', scatter_dimension=...  72.6 us
    reduce_scatter x1, waiting for transfers between devices, local(): lax.psum_scatter(jnp.dot(attended, out_w, preferred_element_type=full_typ...  71 us
    reduce_scatter x1, waiting for transfers between devices, local(): lax.psum_scatter(in_grad.astype(jnp.bfloat16), 'dp', scatter_dimension=0,...  63.8 us
  transfers between devices with their start and end apart: 17, of which 15 were waited for; matrix products, arithmetic and copies ran while one was open for 13% of the time, Pallas kernels for 0%

commit v1 on v0

v1 whole, which is shorter than its diff:
```python
import functools

import jax
import jax.numpy as jnp
from jax import lax
from jax.experimental.layout import Layout, with_layout_constraint
from jax.experimental import pallas as pl
from jax.experimental.pallas import tpu as pltpu
from jax.sharding import PartitionSpec as P

D = 2048
HEAD_DIM = 64
FF = 8192
STEP = 5


EPSILON = 1e-05
ROPE_BASE = 130000.0
BETA_ONE = 0.9
BETA_TWO = 0.95
ADAM_EPSILON = 1e-08
WEIGHT_DECAY = 0.1
GAIN_RATE = 0.5
MASK_VALUE = -1e30

MESH = pl.DeviceIdType.MESH
BF = jnp.bfloat16
F32 = jnp.float32
TILE = 256
LANES = 128
CHUNKS = 2
FINE = 4
FIRST = 4
VMEM_LIMIT = 60 * 1024 * 1024

WHOLE = pl.BlockSpec(memory_space=pltpu.VMEM)
ANY = pl.BlockSpec(memory_space=pl.ANY)


def nn(a, b):
    return lax.dot_general(a, b, (((1,), (0,)), ((), ())), preferred_element_type=F32)


def nt(a, b):
    return lax.dot_general(a, b, (((1,), (1,)), ((), ())), preferred_element_type=F32)


def tn(a, b):
    return lax.dot_general(a, b, (((0,), (0,)), ((), ())), preferred_element_type=F32)


def params(collective_id=None):
    if collective_id is None:
        return pltpu.CompilerParams(vmem_limit_bytes=VMEM_LIMIT)
    return pltpu.CompilerParams(
        vmem_limit_bytes=VMEM_LIMIT, collective_id=collective_id, has_side_effects=True
    )


def cost(microseconds):
    return pl.CostEstimate(
        flops=int(microseconds * 1.0e9), bytes_accessed=int(microseconds * 2.0e6), transcendentals=0
    )


def neighbours(me, n):
    return (me > 0).astype(jnp.int32) + (me < n - 1).astype(jnp.int32)


def chain_barrier(me, n):
    barrier = pltpu.get_barrier_semaphore()
    for there, other in ((me > 0, me - 1), (me < n - 1, me + 1)):

        @pl.when(there)
        def _(other=other):
            pl.semaphore_signal(barrier, inc=1, device_id={"tensor": other}, device_id_type=MESH)

    pl.semaphore_wait(barrier, neighbours(me, n))


def chips_barrier(me, n, line, m):
    chips = m // 2
    chip, core = line // 2, lax.rem(line, 2)
    barrier = pltpu.get_barrier_semaphore()
    for there, other in ((me > 0, me - 1), (me < n - 1, me + 1)):

        @pl.when(there)
        def _(other=other):
            pl.semaphore_signal(barrier, inc=1, device_id={"tensor": other}, device_id_type=MESH)

    pl.semaphore_signal(barrier, inc=1, device_id={"dp": 2 * chip + 1 - core}, device_id_type=MESH)
    for hop in range(1, chips):
        to = 2 * lax.rem(chip + hop, chips) + core
        pl.semaphore_signal(barrier, inc=1, device_id={"dp": to}, device_id_type=MESH)
    pl.semaphore_wait(barrier, neighbours(me, n) + chips)


def everyone_barrier(me, n, line, m):
    barrier = pltpu.get_barrier_semaphore()
    for hop in range(1, n):
        to = lax.rem(me + hop, n)
        pl.semaphore_signal(barrier, inc=1, device_id={"tensor": to}, device_id_type=MESH)
    for hop in range(1, m):
        to = lax.rem(line + hop, m)
        pl.semaphore_signal(barrier, inc=1, device_id={"dp": to}, device_id_type=MESH)
    pl.semaphore_wait(barrier, n + m - 2)


class Gather:
    def __init__(self, me, n, own, place, send, recv, chunks):
        self.me, self.n, self.own, self.place = me, n, own, place
        self.send, self.recv, self.chunks = send, recv, chunks

    def link(self, way, step, c):
        shard = self.me - step if way == 0 else self.me + step
        to = self.me + 1 if way == 0 else self.me - 1
        dst = self.place(shard, c)
        return pltpu.make_async_remote_copy(
            src_ref=self.own(c) if step == 0 else dst,
            dst_ref=dst,
            send_sem=self.send.at[way, step, c],
            recv_sem=self.recv.at[way, step, c],
            device_id={"tensor": to},
            device_id_type=MESH,
        )

    def holds(self, way, step):
        return self.me - step >= 0 if way == 0 else self.me + step <= self.n - 1

    def passes(self, way):
        return self.me < self.n - 1 if way == 0 else self.me > 0

    def start(self):
        for c in range(self.chunks):
            for way in range(2):

                @pl.when(self.passes(way))
                def _(way=way, c=c):
                    self.link(way, 0, c).start()

    def advance(self, step, only=None):
        for c in range(self.chunks) if only is None else (only,):
            for way in range(2):

                @pl.when(self.holds(way, step))
                def _(way=way, c=c):
                    shard = self.me - step if way == 0 else self.me + step
                    here = self.place(shard, c)
                    pltpu.make_async_remote_copy(
                        src_ref=here,
                        dst_ref=here,
                        send_sem=self.send.at[way, step - 1, c],
                        recv_sem=self.recv.at[way, step - 1, c],
                        device_id={"tensor": self.me},
                        device_id_type=MESH,
                    ).wait_recv()
                    if step < self.n - 1:

                        @pl.when(self.passes(way))
                        def _():
                            self.link(way, step, c).start()

    def finish(self):
        for step in range(self.n - 1):
            for c in range(self.chunks):
                for way in range(2):

                    @pl.when(self.holds(way, step) & self.passes(way))
                    def _(way=way, c=c, step=step):
                        self.link(way, step, c).wait_send()


def gather_sems(n, chunks):
    return [pltpu.SemaphoreType.DMA((2, n - 1, chunks)), pltpu.SemaphoreType.DMA((2, n - 1, chunks))]


def nth_dest(me, n, i):
    if i == n - 1:
        return me
    both = jnp.minimum(me, n - 1 - me)
    near = jnp.where((me < n // 2) == (i % 2 == 0), n - 1 - i // 2, i // 2)
    late = i - both
    return jnp.where(i < 2 * both, near, jnp.where(n - 1 - me > me, n - 1 - late, late))


class Scatter:
    def __init__(self, me, n, part, own, inbox, send, recv, chunks):
        self.me, self.n, self.part, self.own, self.inbox = me, n, part, own, inbox
        self.send, self.recv, self.chunks = send, recv, chunks
        self.size = part.shape[1] // chunks
        self.events = (n - 1) * chunks + n - 2

    def rows(self, c):
        return pl.ds(pl.multiple_of(c * self.size, self.size), self.size)

    def box(self, way, step, c):
        return self.inbox.at[step if way == 0 else self.n - step, self.rows(c)]

    def hop(self, way, dest, c):
        step = self.n - 1 - dest if way == 0 else dest
        return pltpu.make_async_remote_copy(
            src_ref=self.part.at[dest, self.rows(c)],
            dst_ref=self.box(way, step, c),
            send_sem=self.send.at[way, step, c],
            recv_sem=self.recv.at[way, step, c],
            device_id={"tensor": self.me + 1 if way == 0 else self.me - 1},
            device_id_type=MESH,
        )

    def offer(self, dest):
        for way in range(2):
            first = (self.me == 0) & (dest > self.me) if way == 0 else (self.me == self.n - 1) & (dest < self.me)

            @pl.when(first)
            def _(way=way):
                for c in range(self.chunks):
                    self.hop(way, dest, c).start()

    def relay(self, time):
        for way in range(2):
            number = time - (self.me - 1) if way == 0 else time - (self.n - 2 - self.me)
            inside = (number >= 0) & (number < (self.n - 1) * self.chunks)
            number = jnp.where(inside, number, 0)
            step = number // self.chunks
            c = number - step * self.chunks
            dest = self.n - 1 - step if way == 0 else step
            if way == 0:
                live = inside & (self.me > 0) & (dest >= self.me)
            else:
                live = inside & (self.me < self.n - 1) & (dest <= self.me)

            @pl.when(live)
            def _(way=way, step=step, c=c, dest=dest):
                here = self.box(way, step, c)
                pltpu.make_async_remote_copy(
                    src_ref=here,
                    dst_ref=here,
                    send_sem=self.send.at[way, step, c],
                    recv_sem=self.recv.at[way, step, c],
                    device_id={"tensor": self.me},
                    device_id_type=MESH,
                ).wait_recv()
                rows = self.rows(c)

                @pl.when(dest == self.me)
                def _():
                    self.own[rows] = self.own[rows] + here[...].astype(F32)

                @pl.when(dest != self.me)
                def _():
                    self.part[dest, rows] = self.part[dest, rows] + here[...]
                    self.hop(way, dest, c).start()

    def relays(self, first, last):
        def body(time, carry):
            self.relay(time)
            return carry

        lax.fori_loop(first, last, body, 0)

    def finish(self):
        for step in range(self.n - 1):
            for c in range(self.chunks):
                for way in range(2):
                    dest = self.n - 1 - step if way == 0 else step

                    @pl.when(self.me < dest if way == 0 else self.me > dest)
                    def _(way=way, dest=dest, c=c):
                        self.hop(way, dest, c).wait_send()


def scatter_scratch(n, rows, width, chunks):
    return [
        pltpu.VMEM((n, rows, width), BF),
        pltpu.VMEM((n + 1, rows, width), BF),
        pltpu.SemaphoreType.DMA((2, n - 1, chunks)),
        pltpu.SemaphoreType.DMA((2, n - 1, chunks)),
    ]


class ChipScatter:
    def __init__(self, line, m, mine, theirs, half, box, pair_send, pair_recv, chip_send, chip_recv):
        self.chips = m // 2
        self.square = self.chips == 4
        self.chip, self.core = line // 2, lax.rem(line, 2)
        self.mine, self.theirs, self.half, self.box = mine, theirs, half, box
        self.pair_send, self.pair_recv = pair_send, pair_recv
        self.chip_send, self.chip_recv = chip_send, chip_recv
        self.kinds, self.size = mine.shape[1], mine.shape[2]
        order = [3, 1, 2, 0] if self.square else list(range(1, self.chips)) + [0]
        self.steps = [(hop, other) for hop in order for other in (True, False)]

    def device(self, hop, core):
        if self.square:
            x, y = lax.rem(self.chip, 2), self.chip // 2
            return 2 * (2 * lax.rem(y + hop // 2, 2) + lax.rem(x + hop % 2, 2)) + core
        return 2 * lax.rem(self.chip + hop, self.chips) + core

    def target(self, at):
        hop, other = self.steps[at]
        return self.device(hop, 1 - self.core if other else self.core)

    def slot(self, at):
        hop, other = self.steps[at]
        return self.theirs.at[hop] if other else self.mine.at[hop]

    def to_pair(self, hop):
        return pltpu.make_async_remote_copy(
            src_ref=self.theirs.at[hop],
            dst_ref=self.half.at[hop],
            send_sem=self.pair_send.at[hop],
            recv_sem=self.pair_recv.at[hop],
            device_id={"dp": 2 * self.chip + 1 - self.core},
            device_id_type=MESH,
        )

    def to_chip(self, hop):
        return pltpu.make_async_remote_copy(
            src_ref=self.mine.at[hop],
            dst_ref=self.box.at[hop],
            send_sem=self.chip_send.at[hop],
            recv_sem=self.chip_recv.at[hop],
            device_id={"dp": self.device(hop, self.core)},
            device_id_type=MESH,
        )

    def over(self, hop):
        rows = pl.ds((hop - 1) * self.size // 2, self.size // 2)
        sem = 3 if hop == 1 else 0
        return pltpu.make_async_remote_copy(
            src_ref=self.mine.at[3, :, rows],
            dst_ref=self.box.at[3, :, rows],
            send_sem=self.chip_send.at[sem],
            recv_sem=self.chip_recv.at[sem],
            device_id={"dp": self.device(hop, self.core)},
            device_id_type=MESH,
        )

    def filled(self, at):
        hop, other = self.steps[at]
        if other:
            self.to_pair(hop).start()
            if at >= 2:
                self.combine(self.steps[at - 1][0])

    def combine(self, hop):
        self.to_pair(hop).wait_recv()
        for kind in range(self.kinds):
            self.mine[hop, kind] = self.mine[hop, kind] + self.half[hop, kind]
        if not self.square:
            if hop > 0:
                self.to_chip(hop).start()
        elif hop == 3:
            self.over(1).start()
            self.over(2).start()

    def forward(self):
        if not self.square:
            return
        for via, hop in ((1, 2), (2, 1)):
            self.over(via).wait_recv()
            rows = pl.ds((via - 1) * self.size // 2, self.size // 2)
            for kind in range(self.kinds):
                self.mine[hop, kind, rows] = self.mine[hop, kind, rows] + self.box[3, kind, rows]
            self.to_chip(hop).start()

    def final(self):
        return (1, 2) if self.square else tuple(range(1, self.chips))

    def arrive(self):
        for hop in self.final():
            self.to_chip(hop).wait_recv()

    def result(self, kind):
        total = self.mine[0, kind].astype(F32)
        for hop in self.final():
            total = total + self.box[hop, kind].astype(F32)
        return total

    def finish(self):
        for hop in range(self.chips):
            self.to_pair(hop).wait_send()
        for hop in self.final():
            self.to_chip(hop).wait_send()
        if self.square:
            self.over(1).wait_send()
            self.over(2).wait_send()


def chip_scatter_scratch(m, shard):
    return [pltpu.VMEM((m // 2,) + shard, BF)] * 4 + [pltpu.SemaphoreType.DMA((m // 2,))] * 4


def half_swap(values):
    lane = lax.broadcasted_iota(jnp.int32, values.shape, 1)
    lower = lax.rem(lane, HEAD_DIM) < HEAD_DIM // 2
    return jnp.where(
        lower, pltpu.roll(values, LANES - HEAD_DIM // 2, 1), pltpu.roll(values, HEAD_DIM // 2, 1)
    )


def row_scale(values):
    return lax.rsqrt(jnp.mean(values * values, axis=-1, keepdims=True) + EPSILON)


def first_kernel(n, m, out_ref, gain_ref, all_out, all_gain, send, recv, gain_send, gain_recv, local_sem):
    me = lax.axis_index("tensor")
    line = lax.axis_index("dp")
    barrier = pltpu.get_barrier_semaphore()
    for hop in range(1, m):
        pl.semaphore_signal(
            barrier, inc=1, device_id={"dp": lax.rem(line + hop, m)}, device_id_type=MESH
        )
    for there, other in ((me > 0, me - 1), (me < n - 1, me + 1)):

        @pl.when(there)
        def _(other=other):
            pl.semaphore_signal(barrier, inc=1, device_id={"tensor": other}, device_id_type=MESH)

    pl.semaphore_wait(barrier, m - 1 + neighbours(me, n))

    size = out_ref.shape[0] // CHUNKS
    gather = Gather(
        me,
        n,
        lambda c: out_ref.at[pl.ds(c * size, size)],
        lambda shard, c: all_out.at[shard, pl.ds(c * size, size)],
        send,
        recv,
        CHUNKS,
    )
    gather.start()

    def gain_copy(hop):
        return pltpu.make_async_remote_copy(
            src_ref=gain_ref,
            dst_ref=all_gain.at[line],
            send_sem=gain_send.at[hop],
            recv_sem=gain_recv.at[hop],
            device_id={"dp": lax.rem(line + hop, m)},
            device_id_type=MESH,
        )

    for hop in range(1, m):
        gain_copy(hop).start()
    mine = pltpu.make_async_copy(out_ref, all_out.at[me], local_sem.at[0])
    mine.start()
    mine_gain = pltpu.make_async_copy(gain_ref, all_gain.at[line], local_sem.at[1])
    mine_gain.start()
    for step in range(1, n):
        gather.advance(step)
    for hop in range(1, m):
        source = lax.rem(line + m - hop, m)
        pltpu.make_async_remote_copy(
            src_ref=gain_ref,
            dst_ref=all_gain.at[source],
            send_sem=gain_send.at[hop],
            recv_sem=gain_recv.at[hop],
            device_id={"dp": source},
            device_id_type=MESH,
        ).wait_recv()
    for hop in range(1, m):
        gain_copy(hop).wait_send()
    gather.finish()
    mine.wait()
    mine_gain.wait()


def gather_first(n, m, out_low, gains):
    rows, width = out_low.shape
    return pl.pallas_call(
        functools.partial(first_kernel, n, m),
        name="gather_out_shards",
        out_shape=(
            jax.ShapeDtypeStruct((n, rows, width), BF),
            jax.ShapeDtypeStruct((m,) + gains.shape, F32),
        ),
        in_specs=[ANY, ANY],
        out_specs=(ANY, ANY),
        scratch_shapes=gather_sems(n, CHUNKS)
        + [
            pltpu.SemaphoreType.DMA((m,)),
            pltpu.SemaphoreType.DMA((m,)),
            pltpu.SemaphoreType.DMA((2,)),
        ],
        compiler_params=params(0),
        cost_estimate=cost(20),
    )(out_low, gains)


def rows_kernel(
    n,
    x_ref,
    up_hbm,
    down_hbm,
    start_ref,
    freq_ref,
    all_x,
    low_ref,
    cos_ref,
    sin_ref,
    send,
    recv,
    up,
    down,
    local_sem,
    load_sem,
):
    me = lax.axis_index("tensor")
    size = x_ref.shape[0] // CHUNKS
    loads = (
        pltpu.make_async_copy(up_hbm, up, load_sem.at[0]),
        pltpu.make_async_copy(down_hbm, down, load_sem.at[1]),
    )
    for copy in loads:
        copy.start()
    chain_barrier(me, n)
    gather = Gather(
        me,
        n,
        lambda c: x_ref.at[pl.ds(c * size, size)],
        lambda shard, c: all_x.at[shard, pl.ds(c * size, size)],
        send,
        recv,
        CHUNKS,
    )
    gather.start()
    mine = pltpu.make_async_copy(x_ref, all_x.at[me], local_sem)
    mine.start()
    for copy in loads:
        copy.wait()
    hidden, each = down.shape

    def cast(r, carry):
        rows = pl.ds(pl.multiple_of(r * 32, 32), 32)
        for kind in range(2):
            low_ref[kind, rows] = up[rows, kind, :].astype(BF)
        return carry

    lax.fori_loop(0, each // 32, cast, 0)

    def turn(c, carry):
        cols = pl.ds(pl.multiple_of(c * TILE, TILE), TILE)
        low_ref[2, :, cols] = jnp.transpose(down[cols]).astype(BF)
        return carry

    lax.fori_loop(0, hidden // TILE, turn, 0)
    gather.advance(1)

    def table(r, carry):
        rows = pl.ds(pl.multiple_of(r * 64, 64), 64)
        place = lax.broadcasted_iota(jnp.int32, (64, LANES), 0) + r * 64 - start_ref[rows]
        lane = lax.broadcasted_iota(jnp.int32, (64, LANES), 1)
        angle = place.astype(F32) * freq_ref[0:1]
        cos_ref[rows] = jnp.cos(angle)
        sine = jnp.sin(angle)
        sin_ref[rows] = jnp.where(lax.rem(lane, HEAD_DIM) < HEAD_DIM // 2, -sine, sine)
        return carry

    lax.fori_loop(0, cos_ref.shape[0] // 64, table, 0)
    for step in range(2, n):
        gather.advance(step)
    gather.finish()
    mine.wait()


def gather_rows(n, x, gate_up, down_weight, starts, freqs):
    each, _, hidden = gate_up.shape
    table = jax.ShapeDtypeStruct(starts.shape, F32)
    return pl.pallas_call(
        functools.partial(rows_kernel, n),
        name="gather_tokens",
        out_shape=(
            jax.ShapeDtypeStruct((n,) + x.shape, BF),
            jax.ShapeDtypeStruct((3, each, hidden), BF),
            table,
            table,
        ),
        in_specs=[ANY] * 3 + [WHOLE] * 2,
        out_specs=(ANY, WHOLE, WHOLE, WHOLE),
        scratch_shapes=gather_sems(n, CHUNKS)
        + [
            pltpu.VMEM(gate_up.shape, F32),
            pltpu.VMEM(down_weight.shape, F32),
            pltpu.SemaphoreType.DMA,
            pltpu.SemaphoreType.DMA((2,)),
        ],
        compiler_params=params(1),
        cost_estimate=cost(65),
    )(x, gate_up, down_weight, starts, freqs)


def attend_kernel(
    n,
    x_hbm,
    gain_ref,
    w_hbm,
    cos_ref,
    sin_ref,
    start_ref,
    back_ref,
    h_hbm,
    qkv_hbm,
    att_hbm,
    lse_ref,
    scale_ref,
    all_back,
    send,
    recv,
    local_sem,
    x_ref,
    w_ref,
    h_ref,
    qkv_ref,
    att_ref,
    move_sem,
):
    me = lax.axis_index("tensor")
    count = x_ref.shape[0]
    width = w_ref.shape[2]
    blocks = count // TILE
    moves = [
        pltpu.make_async_copy(src, dst, move_sem.at[at])
        for at, (src, dst) in enumerate(
            ((x_hbm, x_ref), (w_hbm, w_ref), (h_ref, h_hbm), (qkv_ref, qkv_hbm), (att_ref, att_hbm))
        )
    ]
    moves[0].start()
    moves[1].start()
    size = back_ref.shape[0] // CHUNKS
    chain_barrier(me, n)
    gather = Gather(
        me,
        n,
        lambda c: back_ref.at[pl.ds(c * size, size)],
        lambda shard, c: all_back.at[shard, pl.ds(c * size, size)],
        send,
        recv,
        CHUNKS,
    )
    gather.start()
    mine = pltpu.make_async_copy(back_ref, all_back.at[me], local_sem)
    mine.start()

    def project(r, carry):
        rows = pl.ds(pl.multiple_of(r * TILE, TILE), TILE)
        x = x_ref[rows].astype(F32)
        scale = row_scale(x)
        scale_ref[rows] = jnp.broadcast_to(scale, (TILE, LANES))
        h = (x * scale * gain_ref[0:1]).astype(BF)
        h_ref[rows] = h
        cosine, sine = cos_ref[rows], sin_ref[rows]
        for kind in range(3):
            value = nn(h, w_ref[kind])
            if kind < 2:
                value = jnp.concatenate(
                    [
                        value[:, c : c + LANES] * cosine + half_swap(value[:, c : c + LANES]) * sine
                        for c in range(0, width, LANES)
                    ],
                    axis=1,
                )
            qkv_ref[kind, rows] = value.astype(BF)
        return carry

    moves[0].wait()
    moves[1].wait()
    lax.fori_loop(0, blocks, project, 0)
    moves[2].start()
    moves[3].start()

    lane = lax.broadcasted_iota(jnp.int32, (TILE, LANES), 1)
    key_lane = lax.broadcasted_iota(jnp.int32, (TILE, TILE), 1)
    query_row = lax.broadcasted_iota(jnp.int32, (TILE, TILE), 0)
    diagonal = key_lane <= query_row

    def pair(p, carry):
        cols = pl.ds(pl.multiple_of(p * LANES, LANES), LANES)
        for i in range(blocks):
            rows = pl.ds(i * TILE, TILE)
            query = qkv_ref[0, rows, cols] * jnp.asarray(HEAD_DIM ** (-0.5), BF)
            begin = start_ref[rows, 0:1]
            result = jnp.zeros((TILE, LANES), F32)
            for e in range(2):
                ours = lane < HEAD_DIM if e == 0 else lane >= HEAD_DIM
                q = jnp.where(ours, query, jnp.zeros_like(query))
                scores = []
                for j in range(i + 1):
                    s = nt(q, qkv_ref[1, pl.ds(j * TILE, TILE), cols])
                    allowed = key_lane >= begin - j * TILE
                    if j == i:
                        allowed = allowed & diagonal
                    scores.append(jnp.where(allowed, s, MASK_VALUE))
                top = functools.reduce(jnp.maximum, scores)
                peak = jnp.max(top, axis=-1, keepdims=True)
                expo = [jnp.exp(s - peak) for s in scores]
                total = jnp.sum(functools.reduce(jnp.add, expo), axis=-1, keepdims=True)
                acc = jnp.zeros((TILE, LANES), F32)
                for j in range(i + 1):
                    v = qkv_ref[2, pl.ds(j * TILE, TILE), cols]
                    acc = acc + nn(expo[j].astype(BF), jnp.where(ours, v, jnp.zeros_like(v)))
                result = result + acc / total
                lse = jnp.broadcast_to(peak + jnp.log(total), (TILE, LANES))
                lse_ref[pl.ds(2 * p + e, 1), rows] = jnp.transpose(lse)[0:1]
            att_ref[rows, cols] = result.astype(BF)
        return carry

    pairs = width // LANES
    lax.fori_loop(0, pairs // 2, pair, 0)
    gather.advance(1)
    lax.fori_loop(pairs // 2, pairs, pair, 0)
    moves[4].start()
    for step in range(2, n):
        gather.advance(step)
    gather.finish()
    mine.wait()
    for move in moves[2:]:
        move.wait()


def attend(n, x, gain, weights, cosine, sine, starts, back):
    count, depth = x.shape
    width = weights.shape[2]
    return pl.pallas_call(
        functools.partial(attend_kernel, n),
        name="attention_forward",
        out_shape=(
            jax.ShapeDtypeStruct((count, depth), BF),
            jax.ShapeDtypeStruct((3, count, width), BF),
            jax.ShapeDtypeStruct((count, width), BF),
            jax.ShapeDtypeStruct((width // HEAD_DIM, count), F32),
            jax.ShapeDtypeStruct((count, LANES), F32),
            jax.ShapeDtypeStruct((n,) + back.shape, BF),
        ),
        in_specs=[ANY, WHOLE, ANY, WHOLE, WHOLE, WHOLE, ANY],
        out_specs=(ANY, ANY, ANY, WHOLE, WHOLE, ANY),
        scratch_shapes=gather_sems(n, CHUNKS)
        + [
            pltpu.SemaphoreType.DMA,
            pltpu.VMEM((count, depth), BF),
            pltpu.VMEM(weights.shape, BF),
            pltpu.VMEM((count, depth), BF),
            pltpu.VMEM((3, count, width), BF),
            pltpu.VMEM((count, width), BF),
            pltpu.SemaphoreType.DMA((5,)),
        ],
        compiler_params=params(2),
        cost_estimate=cost(65),
    )(x, gain, weights, cosine, sine, starts, back)


def branch_kernel(
    n, att_ref, w_hbm, x_hbm, gain_ref, h_ref, hidden_ref, held, total, send, recv, w_ref, x_ref, load_sem
):
    me = lax.axis_index("tensor")
    count, width = att_ref.shape
    rows_each = hidden_ref.shape[0]
    size = count // CHUNKS
    loads = (
        pltpu.make_async_copy(w_hbm, w_ref, load_sem.at[0]),
        pltpu.make_async_copy(x_hbm, x_ref, load_sem.at[1]),
    )
    for copy in loads:
        copy.start()
    chain_barrier(me, n)
    gather = Gather(
        me,
        n,
        lambda c: att_ref.at[pl.ds(c * size, size)],
        lambda shard, c: held.at[shard, pl.ds(c * size, size)],
        send,
        recv,
        CHUNKS,
    )
    gather.start()

    def add(source, shard, first, start, stop):
        weights = pl.ds(pl.multiple_of(shard * width, width), width)

        def tile(r, carry):
            rows = pl.ds(pl.multiple_of(r * TILE, TILE), TILE)
            term = nn(source[rows], w_ref[weights])
            total[rows] = term + (x_ref[rows].astype(F32) if first else total[rows])
            return carry

        lax.fori_loop(start // TILE, stop // TILE, tile, 0)

    def arrived(step, start, stop):
        for way in range(2):

            @pl.when(gather.holds(way, step))
            def _(way=way):
                shard = me - step if way == 0 else me + step
                add(held.at[shard], shard, False, start, stop)

    def norm(r, carry):
        rows = pl.ds(pl.multiple_of(r * LANES, LANES), LANES)
        hidden = total[rows]
        h_ref[rows] = (hidden * row_scale(hidden) * gain_ref[1:2]).astype(BF)
        return carry

    for copy in loads:
        copy.wait()
    add(att_ref, me, True, 0, count)
    for step in range(1, n - 1):
        gather.advance(step)
        arrived(step, 0, count)
    for c in range(CHUNKS):
        gather.advance(n - 1, c)
        arrived(n - 1, c * size, (c + 1) * size)
        lax.fori_loop(c * size // LANES, (c + 1) * size // LANES, norm, 0)
    hidden_ref[...] = total[pl.ds(pl.multiple_of(me * rows_each, rows_each), rows_each)]
    gather.finish()


def project_branch(n, att, weights, x, gain):
    count, width = att.shape
    depth = x.shape[1]
    return pl.pallas_call(
        functools.partial(branch_kernel, n),
        name="branch",
        out_shape=(
            jax.ShapeDtypeStruct((count, depth), BF),
            jax.ShapeDtypeStruct((count // n, depth), F32),
        ),
        in_specs=[WHOLE, ANY, ANY, WHOLE],
        out_specs=(WHOLE, WHOLE),
        scratch_shapes=[pltpu.VMEM((n, count, width), BF), pltpu.VMEM((count, depth), F32)]
        + gather_sems(n, CHUNKS)
        + [
            pltpu.VMEM((depth, depth), BF),
            pltpu.VMEM(x.shape, BF),
            pltpu.SemaphoreType.DMA((2,)),
        ],
        compiler_params=params(3),
        cost_estimate=cost(70),
    )(att, weights, x, gain)


def feed_kernel(
    n,
    h_hbm,
    back_hbm,
    w_hbm,
    inner_hbm,
    both_hbm,
    own_ref,
    part,
    inbox,
    send,
    recv,
    w,
    inner_ref,
    both,
    h_rows,
    back_rows,
    w_sem,
    row_sem,
    store_sem,
):
    me = lax.axis_index("tensor")
    rows_each, depth = own_ref.shape
    hidden = inner_ref.shape[1]
    tiles = hidden // TILE
    pair = 2 if tiles % 2 == 0 else 1

    def fetch(b):
        cols = pl.ds(pl.multiple_of(b * TILE, TILE), TILE)
        return pltpu.make_async_copy(w_hbm.at[:, :, cols], w.at[:, :, cols], w_sem.at[b])

    def fetch_rows(dest):
        rows = pl.ds(pl.multiple_of(dest * rows_each, rows_each), rows_each)
        return (
            pltpu.make_async_copy(h_hbm.at[rows], h_rows, row_sem.at[0]),
            pltpu.make_async_copy(back_hbm.at[rows], back_rows, row_sem.at[1]),
        )

    def stores(i, dest):
        rows = pl.ds(pl.multiple_of(dest * rows_each, rows_each), rows_each)
        return (
            pltpu.make_async_copy(inner_ref.at[rows], inner_hbm.at[rows], store_sem.at[i, 0]),
            pltpu.make_async_copy(both.at[:, rows], both_hbm.at[:, rows], store_sem.at[i, 1]),
        )

    for copy in fetch_rows(nth_dest(me, n, 0)):
        copy.start()
    for b in range(tiles):
        fetch(b).start()
    chain_barrier(me, n)
    scatter = Scatter(me, n, part, own_ref, inbox, send, recv, FINE)
    own_ref[...] = jnp.zeros_like(own_ref)
    step_cols = 512
    steps = tiles // pair
    per_block = steps + depth // step_cols
    last = n * per_block
    due = [last + 1] * scatter.events
    if n == 4 and per_block == 8:
        due = [11, 16, 17, 19, 24, 25, 26, 28, 31] + due[9:]

    def serve(tick):
        def count(now):
            return functools.reduce(jnp.add, [(now >= at).astype(jnp.int32) for at in due])

        scatter.relays(count(tick - 1), count(tick))

    for i in range(n):
        dest = nth_dest(me, n, i)
        rows = pl.ds(pl.multiple_of(dest * rows_each, rows_each), rows_each)
        for copy in fetch_rows(dest):
            copy.wait()

        def forward(b, carry, i=i, rows=rows):
            if i == 0:
                for half in range(pair):
                    fetch(pair * b + half).wait()
            for half in range(pair):
                cols = pl.ds(pl.multiple_of((pair * b + half) * TILE, TILE), TILE)
                gate = nn(h_rows[...], w[0, :, cols])
                up = nn(h_rows[...], w[1, :, cols])
                d_inner = nn(back_rows[...], w[2, :, cols])
                sigmoid = jax.nn.sigmoid(gate)
                silu = gate * sigmoid
                inner_ref[rows, cols] = (silu * up).astype(BF)
                both[0, rows, cols] = (d_inner * up * sigmoid * (1.0 + gate * (1.0 - sigmoid))).astype(BF)
                both[1, rows, cols] = (d_inner * silu).astype(BF)
            if i > 0:
                serve(i * per_block + 1 + b)
            return carry

        lax.fori_loop(0, steps, forward, 0)
        if i < n - 1:
            for copy in fetch_rows(nth_dest(me, n, i + 1)):
                copy.start()
        for copy in stores(i, dest):
            copy.start()

        def backward(c, carry, i=i, rows=rows, dest=dest):
            cols = pl.ds(pl.multiple_of(c * step_cols, step_cols), step_cols)
            value = nt(both[0, rows], w[0, cols]) + nt(both[1, rows], w[1, cols])
            if i < n - 1:
                part[dest, :, cols] = value.astype(BF)
            else:
                own_ref[:, cols] = own_ref[:, cols] + value
            if i > 0:
                serve(i * per_block + steps + 1 + c)
            return carry

        lax.fori_loop(0, depth // step_cols, backward, 0)
        if i < n - 1:
            scatter.offer(dest)

    late = [at for at in range(scatter.events) if due[at] > last]
    scatter.relays(late[0], scatter.events)
    for i in range(n):
        for copy in stores(i, nth_dest(me, n, i)):
            copy.wait()
    scatter.finish()


def feed(n, h, back, weights):
    count, depth = h.shape
    hidden = weights.shape[2]
    rows = count // n
    return pl.pallas_call(
        functools.partial(feed_kernel, n),
        name="feed_forward",
        out_shape=(
            jax.ShapeDtypeStruct((count, hidden), BF),
            jax.ShapeDtypeStruct((2, count, hidden), BF),
            jax.ShapeDtypeStruct((rows, depth), F32),
        ),
        in_specs=[ANY] * 3,
        out_specs=(ANY, ANY, WHOLE),
        scratch_shapes=scatter_scratch(n, rows, depth, FINE)
        + [
            pltpu.VMEM((3, depth, hidden), BF),
            pltpu.VMEM((count, hidden), BF),
            pltpu.VMEM((2, count, hidden), BF),
            pltpu.VMEM((rows, depth), BF),
            pltpu.VMEM((rows, depth), BF),
            pltpu.SemaphoreType.DMA((hidden // TILE,)),
            pltpu.SemaphoreType.DMA((2,)),
            pltpu.SemaphoreType.DMA((n, 2)),
        ],
        compiler_params=params(4),
        cost_estimate=cost(95),
    )(h, back, weights)


def branch_back_kernel(
    n,
    m,
    d_two_ref,
    hidden_ref,
    cot_ref,
    gain_ref,
    w_hbm,
    h_hbm,
    both_hbm,
    back_hbm,
    inner_hbm,
    feed_hbm,
    d_hidden_ref,
    d_att_ref,
    gain_part_ref,
    all_hbm,
    grad_hbm,
    down_ref,
    first_ref,
    held,
    w_ref,
    send,
    recv,
    w_sem,
    out_sem,
    both,
    inner,
    h_cols,
    back_cols,
    slot,
    both_sem,
    col_sem,
    slot_sem,
    down,
    part,
    inbox,
    s_send,
    s_recv,
    *chip_scratch,
):
    me = lax.axis_index("tensor")
    line = lax.axis_index("dp")
    down_sum = ChipScatter(line, m, *chip_scratch)
    rows_each, depth = hidden_ref.shape
    width = d_att_ref.shape[1]
    size = rows_each // CHUNKS
    fetch = pltpu.make_async_copy(
        w_hbm.at[pl.ds(pl.multiple_of(me * width, width), width)], w_ref, w_sem
    )
    fetch.start()
    loads = (
        pltpu.make_async_copy(inner_hbm, inner, both_sem.at[0]),
        pltpu.make_async_copy(feed_hbm.at[2, pl.ds(0, down.shape[0])], down, both_sem.at[1]),
        pltpu.make_async_copy(both_hbm, both, both_sem.at[2]),
    )
    for copy in loads:
        copy.start()
    each = depth // m

    def fetch_cols(at):
        cols = pl.ds(pl.multiple_of(at * each, each), each)
        to = lax.rem(at, 2)
        return pltpu.make_async_copy(h_hbm.at[:, cols], h_cols.at[to], col_sem.at[0, to])

    def fetch_back(at):
        cols = pl.ds(pl.multiple_of(down_sum.target(at) * each, each), each)
        return pltpu.make_async_copy(back_hbm.at[:, cols], back_cols.at[at % 2], col_sem.at[1, at % 2])

    fetch_cols(0).start()
    fetch_back(0).start()
    chips_barrier(me, n, line, m)
    step_rows = min(LANES, rows_each)
    gain_part_ref[...] = jnp.zeros_like(gain_part_ref)

    def norm(r, carry):
        rows = pl.ds(pl.multiple_of(r * step_rows, step_rows), step_rows)
        hidden = hidden_ref[rows]
        scale = row_scale(hidden)
        normed = hidden * scale
        d_two = d_two_ref[rows]
        scaled = d_two * gain_ref[1:2]
        back = scale * (scaled - normed * jnp.mean(scaled * normed, axis=-1, keepdims=True))
        d_hidden = cot_ref[rows].astype(F32) + back
        d_hidden_ref[rows] = d_hidden
        held[me, rows] = d_hidden.astype(BF)
        gain_part_ref[1:2] = gain_part_ref[1:2] + jnp.sum(d_two * normed, axis=0, keepdims=True)
        return carry

    lax.fori_loop(0, rows_each // step_rows, norm, 0)

    gather = Gather(
        me,
        n,
        lambda c: held.at[me, pl.ds(c * size, size)],
        lambda shard, c: held.at[shard, pl.ds(c * size, size)],
        send,
        recv,
        CHUNKS,
    )
    gather.start()

    def use(shard):
        rows = pl.ds(pl.multiple_of(shard * rows_each, rows_each), rows_each)
        pltpu.make_async_copy(held.at[shard], all_hbm.at[shard], out_sem.at[shard]).start()
        d_att_ref[rows] = nt(held[shard], w_ref[...]).astype(BF)

    def out_copy(at, kind):
        return pltpu.make_async_copy(slot.at[kind], grad_hbm.at[2 * at + kind], slot_sem.at[kind])

    step_cols = 512
    tiles = inner.shape[1] // step_cols

    def up_piece(at, carry):
        @pl.when(at + 1 < m)
        def _():
            fetch_cols(at + 1).start()

        fetch_cols(at).wait()
        turned = jnp.transpose(h_cols[lax.rem(at, 2)])
        for kind in range(2):

            @pl.when(at > 0)
            def _(kind=kind):
                out_copy(at - 1, kind).wait()

            def tile(c, inner_carry, kind=kind):
                cols = pl.ds(pl.multiple_of(c * step_cols, step_cols), step_cols)
                slot[kind, :, cols] = nn(turned, both[kind, :, cols]).astype(BF)
                return inner_carry

            lax.fori_loop(0, tiles, tile, 0)
            out_copy(at, kind).start()
        return carry

    def down_piece(at):
        if at + 1 < m:
            fetch_back(at + 1).start()
        fetch_back(at).wait()
        turned = jnp.transpose(back_cols[at % 2])
        to = down_sum.slot(at)

        def tile(c, carry):
            cols = pl.ds(pl.multiple_of(c * step_cols, step_cols), step_cols)
            to[0, :, cols] = nn(turned, inner[:, cols]).astype(BF)
            return carry

        lax.fori_loop(0, tiles, tile, 0)
        down_sum.filled(at)

    scatter = Scatter(me, n, part, first_ref, inbox, s_send, s_recv, CHUNKS)
    first_ref[...] = hidden_ref[:, 0 : first_ref.shape[1]]
    loads[0].wait()
    loads[1].wait()
    for i in range(n):
        dest = nth_dest(me, n, i)
        rows = pl.ds(pl.multiple_of(dest * rows_each, rows_each), rows_each)
        value = nt(inner[rows], down[...])
        if i < n - 1:
            part[dest] = value.astype(BF)
            scatter.offer(dest)
        else:
            first_ref[...] = first_ref[...] + value
    for at in range(m):
        down_piece(at)
    fetch.wait()
    use(me)
    down_sum.combine(0)
    down_sum.forward()
    loads[2].wait()

    def arrived(step):
        for way in range(2):

            @pl.when(gather.holds(way, step))
            def _(way=way):
                use(me - step if way == 0 else me + step)

    gather.advance(1)
    arrived(1)
    lax.fori_loop(0, m // 2, up_piece, 0)
    gather.advance(2)
    arrived(2)
    lax.fori_loop(m // 2, m, up_piece, 0)
    scatter.relays(0, scatter.events)
    down_sum.arrive()
    down_ref[...] = jnp.transpose(down_sum.result(0))
    for step in range(3, n):
        gather.advance(step)
        arrived(step)
    for kind in range(2):
        out_copy(m - 1, kind).wait()
    for shard in range(n):
        pltpu.make_async_copy(held.at[shard], all_hbm.at[shard], out_sem.at[shard]).wait()
    gather.finish()
    scatter.finish()
    down_sum.finish()


def branch_back(n, m, d_two, hidden, cotangent, gain, out_weights, h, both, back, inner, feed_weights, width):
    rows, depth = hidden.shape
    _, count, inner_width = both.shape
    each = depth // m
    first = depth // FIRST
    return pl.pallas_call(
        functools.partial(branch_back_kernel, n, m),
        name="branch_backward",
        out_shape=(
            jax.ShapeDtypeStruct((rows, depth), F32),
            jax.ShapeDtypeStruct((n * rows, width), BF),
            jax.ShapeDtypeStruct((8, depth), F32),
            jax.ShapeDtypeStruct((n, rows, depth), BF),
            jax.ShapeDtypeStruct((2 * m, each, inner_width), BF),
            jax.ShapeDtypeStruct((inner_width, each), F32),
            jax.ShapeDtypeStruct((rows, first), F32),
        ),
        in_specs=[WHOLE] * 4 + [ANY] * 6,
        out_specs=(WHOLE, WHOLE, WHOLE, ANY, ANY, WHOLE, WHOLE),
        scratch_shapes=[pltpu.VMEM((n, rows, depth), BF), pltpu.VMEM((width, depth), BF)]
        + gather_sems(n, CHUNKS)
        + [
            pltpu.SemaphoreType.DMA,
            pltpu.SemaphoreType.DMA((n,)),
            pltpu.VMEM(both.shape, BF),
            pltpu.VMEM(inner.shape, BF),
            pltpu.VMEM((2, count, each), BF),
            pltpu.VMEM((2, count, each), BF),
            pltpu.VMEM((2, each, inner_width), BF),
            pltpu.SemaphoreType.DMA((3,)),
            pltpu.SemaphoreType.DMA((2, 2)),
            pltpu.SemaphoreType.DMA((2,)),
            pltpu.VMEM((first, inner_width), BF),
        ]
        + scatter_scratch(n, rows, first, CHUNKS)
        + chip_scatter_scratch(m, (1, each, inner_width)),
        compiler_params=params(5),
        cost_estimate=cost(75),
    )(d_two, hidden, cotangent, gain, out_weights, h, both, back, inner, feed_weights)


def attend_back_kernel(
    n,
    lse_ref,
    start_ref,
    qkv_hbm,
    d_att_hbm,
    cos_hbm,
    sin_hbm,
    hidden_hbm,
    inner_hbm,
    w_hbm,
    first_ref,
    d_hbm,
    out_ref,
    part,
    inbox,
    send,
    recv,
    own,
    inner,
    down,
    key_sum,
    value_sum,
    load_sem,
    qkv_ref,
    d_att_ref,
    cos_ref,
    sin_ref,
    d_ref,
    store_sem,
):
    me = lax.axis_index("tensor")
    count, width = d_att_ref.shape
    rows_each, depth = out_ref.shape
    first = first_ref.shape[1]
    blocks = count // TILE
    loads = [
        pltpu.make_async_copy(src, dst, load_sem.at[at])
        for at, (src, dst) in enumerate(
            (
                (hidden_hbm.at[:, pl.ds(first, depth - first)], own),
                (inner_hbm, inner),
                (w_hbm.at[2, pl.ds(first, depth - first)], down),
                (qkv_hbm, qkv_ref),
                (d_att_hbm, d_att_ref),
                (cos_hbm, cos_ref),
                (sin_hbm, sin_ref),
            )
        )
    ]
    for copy in loads:
        copy.start()

    chain_barrier(me, n)
    scatter = Scatter(me, n, part, own, inbox, send, recv, FINE)
    for copy in loads[:3]:
        copy.wait()
    step_cols = 512
    for i in range(n):
        dest = nth_dest(me, n, i)

        def tile(c, carry, i=i, dest=dest):
            rows = pl.ds(pl.multiple_of(dest * rows_each, rows_each), rows_each)
            cols = pl.ds(pl.multiple_of(c * step_cols, step_cols), step_cols)
            value = nt(inner[rows], down[cols])
            if i < n - 1:
                part[dest, :, cols] = value.astype(BF)
            else:
                own[:, cols] = own[:, cols] + value
            return carry

        lax.fori_loop(0, (depth - first) // step_cols, tile, 0)
        if i < n - 1:
            scatter.offer(dest)
    for copy in loads[3:]:
        copy.wait()

    lane = lax.broadcasted_iota(jnp.int32, (TILE, LANES), 1)
    key_row = lax.broadcasted_iota(jnp.int32, (TILE, TILE), 0)
    query_lane = lax.broadcasted_iota(jnp.int32, (TILE, TILE), 1)
    diagonal = key_row <= query_lane
    scale = HEAD_DIM ** (-0.5)

    def unrotate(value, rows):
        return value * cos_ref[rows] - half_swap(value) * sin_ref[rows]

    def pair(p, carry):
        cols = pl.ds(pl.multiple_of(p * LANES, LANES), LANES)
        key_sum[...] = jnp.zeros_like(key_sum)
        value_sum[...] = jnp.zeros_like(value_sum)
        for i in range(blocks):
            rows = pl.ds(i * TILE, TILE)
            query = qkv_ref[0, rows, cols] * jnp.asarray(scale, BF)
            back = d_att_ref[rows, cols]
            begin = start_ref[0:1, rows]
            query_grad = jnp.zeros((TILE, LANES), F32)
            for e in range(2):
                ours = lane < HEAD_DIM if e == 0 else lane >= HEAD_DIM
                q = jnp.where(ours, query, jnp.zeros_like(query))
                d = jnp.where(ours, back, jnp.zeros_like(back))
                lse = lse_ref[pl.ds(2 * p + e, 1), rows]
                probs, d_probs = [], []
                centre = jnp.zeros((1, TILE), F32)
                for j in range(i + 1):
                    keys = pl.ds(j * TILE, TILE)
                    s = nt(qkv_ref[1, keys, cols], q)
                    allowed = key_row >= begin - j * TILE
                    if j == i:
                        allowed = allowed & diagonal
                    prob = jnp.where(allowed, jnp.exp(s - lse), 0.0)
                    d_prob = nt(qkv_ref[2, keys, cols], d)
                    centre = centre + jnp.sum(prob * d_prob, axis=0, keepdims=True)
                    value_sum[keys] = value_sum[keys] + nn(prob.astype(BF), d)
                    probs.append(prob)
                    d_probs.append(d_prob)
                for j in range(i + 1):
                    keys = pl.ds(j * TILE, TILE)
                    d_score = (probs[j] * (d_probs[j] - centre)).astype(BF)
                    key_sum[keys] = key_sum[keys] + nn(d_score, q)
                    k = qkv_ref[1, keys, cols]
                    query_grad = query_grad + tn(d_score, jnp.where(ours, k, jnp.zeros_like(k)))
            d_ref[0, rows, cols] = unrotate(query_grad * scale, rows).astype(BF)
            if i == blocks // 2 - 1:
                scatter.relays(5 * p // 2, 5 * p // 2 + 1)
            if i == blocks // 2:
                scatter.relays(5 * p // 2 + 1, 5 * (p + 1) // 2 - 1)
        for i in range(blocks):
            rows = pl.ds(i * TILE, TILE)
            d_ref[1, rows, cols] = unrotate(key_sum[rows], rows).astype(BF)
            d_ref[2, rows, cols] = value_sum[rows].astype(BF)
        scatter.relays(5 * (p + 1) // 2 - 1, 5 * (p + 1) // 2)
        return carry

    pairs = width // LANES
    lax.fori_loop(0, pairs, pair, 0)
    done = 5 * pairs // 2

    store = pltpu.make_async_copy(d_ref, d_hbm, store_sem)
    store.start()
    scatter.relays(done, scatter.events)
    out_ref[:, 0:first] = first_ref[...].astype(BF)
    out_ref[:, first:depth] = own[...].astype(BF)
    scatter.finish()
    store.wait()


def attend_back(n, qkv, d_att, lse, starts, cosine, sine, hidden, inner, weights, feed_first):
    _, count, width = qkv.shape
    rows, depth = hidden.shape
    inner_width = inner.shape[1]
    rest = depth - feed_first.shape[1]
    return pl.pallas_call(
        functools.partial(attend_back_kernel, n),
        name="attention_backward",
        out_shape=(
            jax.ShapeDtypeStruct((3, count, width), BF),
            jax.ShapeDtypeStruct((rows, depth), BF),
        ),
        in_specs=[WHOLE] * 2 + [ANY] * 7 + [WHOLE],
        out_specs=(ANY, WHOLE),
        scratch_shapes=scatter_scratch(n, rows, rest, FINE)
        + [
            pltpu.VMEM((rows, rest), F32),
            pltpu.VMEM((count, inner_width), BF),
            pltpu.VMEM((rest, inner_width), BF),
            pltpu.VMEM((count, LANES), F32),
            pltpu.VMEM((count, LANES), F32),
            pltpu.SemaphoreType.DMA((7,)),
            pltpu.VMEM(qkv.shape, BF),
            pltpu.VMEM(d_att.shape, BF),
            pltpu.VMEM(cosine.shape, F32),
            pltpu.VMEM(sine.shape, F32),
            pltpu.VMEM(qkv.shape, BF),
            pltpu.SemaphoreType.DMA,
        ],
        compiler_params=params(6),
        cost_estimate=cost(80),
    )(
        lse,
        starts,
        qkv,
        d_att,
        cosine,
        sine,
        hidden,
        inner,
        weights,
        feed_first,
    )


def input_back_kernel(
    n,
    m,
    d_ref,
    w_ref,
    x_ref,
    gain_ref,
    d_hidden_ref,
    gain_two_ref,
    scale_ref,
    all_x_hbm,
    h_hbm,
    branch_hbm,
    att_hbm,
    grad_ref,
    in_ref,
    out_ref,
    gain_ref_out,
    part,
    inbox,
    send,
    recv,
    own,
    gain_part,
    t_box,
    line_sum,
    d_box,
    t_send,
    t_recv,
    d_send,
    d_recv,
    att,
    h_cols,
    branch_cols,
    all_x,
    att_sem,
    x_sem,
    col_sem,
    *chip_scratch,
):
    me = lax.axis_index("tensor")
    line = lax.axis_index("dp")
    rows_each, depth = x_ref.shape
    kinds = in_ref.shape[0] + 1
    mixed_sum = ChipScatter(line, m, *chip_scratch)
    each = in_ref.shape[1]
    fetch_att = pltpu.make_async_copy(att_hbm, att, att_sem)
    fetch_x = pltpu.make_async_copy(all_x_hbm, all_x, x_sem)
    fetch_x.start()
    fetch_att.start()

    def fetch_cols(at):
        cols = pl.ds(pl.multiple_of(mixed_sum.target(at) * each, each), each)
        return (
            pltpu.make_async_copy(h_hbm.at[:, cols], h_cols.at[at % 2], col_sem.at[0, at % 2]),
            pltpu.make_async_copy(branch_hbm.at[:, cols], branch_cols.at[at % 2], col_sem.at[1, at % 2]),
        )

    for copy in fetch_cols(0):
        copy.start()
    everyone_barrier(me, n, line, m)
    scatter = Scatter(me, n, part, own, inbox, send, recv, FINE)
    own[...] = jnp.zeros_like(own)
    gain_part[...] = gain_two_ref[...]
    fetch_x.wait()
    step_cols = 512

    def term(i):
        dest = nth_dest(me, n, i)

        def tile(c, carry):
            rows = pl.ds(pl.multiple_of(dest * rows_each, rows_each), rows_each)
            cols = pl.ds(pl.multiple_of(c * step_cols, step_cols), step_cols)
            value = nt(d_ref[0, rows], w_ref[0, cols])
            for kind in range(1, 3):
                value = value + nt(d_ref[kind, rows], w_ref[kind, cols])
            if i < n - 1:
                part[dest, :, cols] = value.astype(BF)
            else:
                own[:, cols] = own[:, cols] + value
            normed = all_x[rows, cols].astype(F32) * scale_ref[rows, 0:1]
            gain_part[0:1, cols] = gain_part[0:1, cols] + jnp.sum(value * normed, axis=0, keepdims=True)
            return carry

        lax.fori_loop(0, depth // step_cols, tile, 0)
        if i < n - 1:
            scatter.offer(dest)

    term(0)
    term(1)
    def across(hop):
        return pltpu.make_async_remote_copy(
            src_ref=gain_part,
            dst_ref=t_box.at[hop],
            send_sem=t_send.at[hop],
            recv_sem=t_recv.at[hop],
            device_id={"tensor": lax.rem(me + hop, n)},
            device_id_type=MESH,
        )

    def along(hop):
        to = lax.rem(line + hop, m)
        return pltpu.make_async_remote_copy(
            src_ref=line_sum.at[to],
            dst_ref=d_box.at[hop],
            send_sem=d_send.at[hop],
            recv_sem=d_recv.at[hop],
            device_id={"dp": to},
            device_id_type=MESH,
        )

    fetch_att.wait()
    served = 0
    for at in range(m):
        if at + 1 < m:
            for copy in fetch_cols(at + 1):
                copy.start()
        for copy in fetch_cols(at):
            copy.wait()
        h_turned = jnp.transpose(h_cols[at % 2])
        branch_turned = jnp.transpose(branch_cols[at % 2])
        to = mixed_sum.slot(at)
        for kind in range(kinds):
            value = nn(h_turned, d_ref[kind]) if kind < kinds - 1 else nn(branch_turned, att[...])
            to[kind] = value.astype(BF)
        mixed_sum.filled(at)
        if 4 * (at + 1) // m - 1 > served:
            scatter.relay(served)
            served += 1
    mixed_sum.combine(0)
    for i in range(2, n):
        term(i)
    for hop in range(1, n):
        across(hop).start()
    scatter.relays(served, served + 1)
    mixed_sum.forward()
    scatter.relays(served + 1, served + 3)
    for hop in range(1, n):
        across(hop).wait_recv()
    gain_total = gain_part[...]
    for hop in range(1, n):
        gain_total = gain_total + t_box[hop]
    gain_width = gain_ref_out.shape[1]
    for at in range(m):
        line_sum[at] = gain_total[:, at * gain_width : (at + 1) * gain_width]
    for hop in range(1, m):
        along(hop).start()
    scatter.relays(served + 3, scatter.events)
    step_rows = min(LANES, rows_each)

    def norm(r, carry):
        rows = pl.ds(pl.multiple_of(r * step_rows, step_rows), step_rows)
        x = x_ref[rows].astype(F32)
        scale = row_scale(x)
        normed = x * scale
        d_one = own[rows]
        scaled = d_one * gain_ref[0:1]
        back = scale * (scaled - normed * jnp.mean(scaled * normed, axis=-1, keepdims=True))
        grad_ref[rows] = d_hidden_ref[rows] + back
        return carry

    lax.fori_loop(0, rows_each // step_rows, norm, 0)
    for hop in range(1, m):
        along(hop).wait_recv()
    result = line_sum[line]
    for hop in range(1, m):
        result = result + d_box[hop]
    gain_ref_out[...] = result
    mixed_sum.arrive()
    for kind in range(kinds):
        total = mixed_sum.result(kind)
        if kind < kinds - 1:
            in_ref[kind] = total
        else:
            out_ref[...] = jnp.transpose(total)

    scatter.finish()
    for hop in range(1, n):
        across(hop).wait_send()
    for hop in range(1, m):
        along(hop).wait_send()
    mixed_sum.finish()


def input_back(
    n, m, d_projected, weights, x, gain, d_hidden, gain_two, scale, all_x, h, d_branch, attended
):
    rows, depth = x.shape
    kinds = d_projected.shape[0] + 1
    each = depth // m
    count, width = attended.shape
    shard = (kinds, each, width)
    return pl.pallas_call(
        functools.partial(input_back_kernel, n, m),
        name="input_backward",
        out_shape=(
            jax.ShapeDtypeStruct((rows, depth), F32),
            jax.ShapeDtypeStruct((kinds - 1, each, width), F32),
            jax.ShapeDtypeStruct((width, each), F32),
            jax.ShapeDtypeStruct((8, each), F32),
        ),
        in_specs=[WHOLE] * 7 + [ANY] * 4,
        out_specs=(WHOLE,) * 4,
        scratch_shapes=scatter_scratch(n, rows, depth, FINE)
        + [pltpu.VMEM((rows, depth), F32)]
        + [
            pltpu.VMEM((8, depth), F32),
            pltpu.VMEM((n, 8, depth), F32),
            pltpu.VMEM((m, 8, each), F32),
            pltpu.VMEM((m, 8, each), F32),
            pltpu.SemaphoreType.DMA((n,)),
            pltpu.SemaphoreType.DMA((n,)),
            pltpu.SemaphoreType.DMA((m,)),
            pltpu.SemaphoreType.DMA((m,)),
            pltpu.VMEM((count, width), BF),
            pltpu.VMEM((2, count, each), BF),
            pltpu.VMEM((2, count, each), BF),
            pltpu.VMEM((count, depth), BF),
            pltpu.SemaphoreType.DMA,
            pltpu.SemaphoreType.DMA,
            pltpu.SemaphoreType.DMA((2, 2)),
        ]
        + chip_scatter_scratch(m, shard),
        compiler_params=params(7),
        cost_estimate=cost(75),
    )(
        d_projected,
        weights,
        x,
        gain,
        d_hidden,
        gain_two,
        scale,
        all_x,
        h,
        d_branch,
        attended,
    )


def adam_kernel(rate, decay, w_ref, first_ref, second_ref, grad_ref, first_out, second_out, w_out):
    for kind in range(2):
        new = adam_step(
            w_ref[:, kind, :],
            first_ref[:, kind, :],
            second_ref[:, kind, :],
            grad_ref[kind].astype(F32),
            rate,
            decay,
        )
        first_out[:, kind, :] = new[0]
        second_out[:, kind, :] = new[1]
        w_out[:, kind, :] = new[2]


def adam_pair(weight, first, second, grad, rate, decay):
    rows, kinds, width = weight.shape
    step = 64
    spec = pl.BlockSpec((step, kinds, width), lambda i: (i, 0, 0))
    shape = jax.ShapeDtypeStruct(weight.shape, F32)
    return pl.pallas_call(
        functools.partial(adam_kernel, rate, decay),
        name="adam_gate_up",
        grid=(rows // step,),
        out_shape=(shape,) * 3,
        in_specs=[spec] * 3 + [pl.BlockSpec((kinds, step, width), lambda i: (0, i, 0))],
        out_specs=(spec,) * 3,
        compiler_params=params(),
        cost_estimate=cost(10),
    )(weight, first, second, grad)


def rows_first(array):
    return with_layout_constraint(array, Layout(major_to_minor=tuple(range(array.ndim))))


def adam_step(weight, first_moment, second_moment, grad, rate, decay):
    new_first = BETA_ONE * first_moment + (1.0 - BETA_ONE) * grad
    new_second = BETA_TWO * second_moment + (1.0 - BETA_TWO) * grad * grad
    mean_part = new_first / (1.0 - BETA_ONE**STEP)
    size_part = jnp.sqrt(new_second / (1.0 - BETA_TWO**STEP)) + ADAM_EPSILON
    new_weight = weight - rate * (mean_part / size_part + decay * weight)
    return (new_first, new_second, new_weight)


def local(
    n,
    m,
    tokens,
    cotangent,
    doc_start,
    in_weight,
    in_first,
    in_second,
    out_weight,
    out_first,
    out_second,
    gate_up,
    gate_up_first,
    gate_up_second,
    down_weight,
    down_first,
    down_second,
    norm_gains,
    gains_first,
    gains_second,
):
    count = doc_start.shape[0]
    depth = tokens.shape[1]

    in_low = jnp.transpose(in_weight, (1, 0, 2)).astype(BF)
    gain_low = jnp.pad(lax.reduce_precision(norm_gains, 8, 7), ((0, 6), (0, 0)))
    powers = jnp.arange(HEAD_DIM // 2, dtype=F32) * (2.0 / HEAD_DIM)
    freqs = jnp.broadcast_to(jnp.tile(ROPE_BASE ** (-powers), 4)[None, :], (8, LANES))
    start_rows = jnp.broadcast_to(doc_start[:, None], (count, LANES))
    start_lanes = jnp.broadcast_to(doc_start[None, :], (8, count))

    in_w = lax.all_gather(in_low, "dp", axis=1, tiled=True)
    out_line, gain_line = gather_first(n, m, out_weight.astype(BF), gain_low)
    gains = jnp.transpose(gain_line, (1, 0, 2)).reshape(8, depth)
    out_line = out_line.reshape(depth, out_line.shape[2])
    out_w = lax.all_gather(out_line, "dp", axis=1, tiled=True)

    own_tokens, _ = lax.optimization_barrier((tokens, gains))
    x, feed_low, cosine, sine = gather_rows(n, own_tokens, gate_up, down_weight, start_rows, freqs)
    x = x.reshape(count, depth)
    feed_w = lax.all_gather(feed_low, "dp", axis=1, tiled=True)

    h_one, qkv, attended, lse, scale_one, back = attend(
        n, x, gains, in_w, cosine, sine, start_rows, cotangent
    )
    back = back.reshape(count, depth)
    h_two, hidden = project_branch(n, attended, out_w, x, gains)
    inner, d_both, d_two = feed(n, h_two, back, feed_w)
    d_hidden, d_att, gain_two, d_branch, up_grad, down_summed, feed_first = branch_back(
        n,
        m,
        d_two,
        hidden,
        cotangent,
        gains,
        out_w,
        h_two,
        d_both,
        back,
        inner,
        feed_w,
        attended.shape[1],
    )
    up_summed = rows_first(lax.psum_scatter(up_grad, "dp", scatter_dimension=0, tiled=True))
    d_projected, output = attend_back(
        n, qkv, d_att, lse, start_lanes, cosine, sine, hidden, inner, feed_w, feed_first
    )
    input_grad, in_summed, out_summed, gain_summed = input_back(
        n,
        m,
        d_projected,
        in_w,
        tokens,
        gains,
        d_hidden,
        gain_two,
        scale_one,
        x,
        h_one,
        d_branch.reshape(count, depth),
        attended,
    )
    up_new = tuple(
        adam_pair(
            gate_up, gate_up_first, gate_up_second, up_summed, 2.0 * D ** (-0.5), WEIGHT_DECAY
        )
    )
    down_new = adam_step(
        down_weight, down_first, down_second, down_summed, 2.0 * FF ** (-0.5), WEIGHT_DECAY
    )
    in_new = adam_step(
        in_weight, in_first, in_second, jnp.transpose(in_summed, (1, 0, 2)), 2.0 * D ** (-0.5), WEIGHT_DECAY
    )
    out_new = adam_step(
        out_weight, out_first, out_second, out_summed, 2.0 * (D // 8) ** (-0.5), WEIGHT_DECAY
    )
    gain_new = adam_step(norm_gains, gains_first, gains_second, gain_summed[0:2], GAIN_RATE, 0.0)
    return (output, input_grad) + in_new + out_new + up_new + down_new + gain_new


def solution(mesh):
    rows = P(("dp", "tensor"), None)
    wide = P("dp", None, "tensor")
    tall = P("tensor", "dp")
    gains = P(None, "dp")
    in_specs = (rows, rows, P("dp")) + (wide,) * 3 + (tall,) * 3 + (wide,) * 3 + (tall,) * 3 + (gains,) * 3
    out_specs = (rows, rows) + (wide,) * 3 + (tall,) * 3 + (wide,) * 3 + (tall,) * 3 + (gains,) * 3
    return jax.shard_map(
        functools.partial(local, mesh.shape["tensor"], mesh.shape["dp"]),
        mesh=mesh,
        in_specs=in_specs,
        out_specs=out_specs,
        check_vma=False,
    )
```

time: 1480 us -> 641 us (0.43)
  waiting for transfers between devices: 990 us -> 0.13 us
  Pallas kernels: 0 us -> 599 us
  matrix products: 301 us -> 0 us
  local copies, waits for them, and re-layouts: 71.2 us -> 7.91 us
  other arithmetic: 75.7 us -> 15.4 us
  blocking collectives: 23.6 us -> 0 us
    pallas_call x0 -> x9, Pallas kernels: none -> 599 us  [the longest x1 96.5 us: branch_back(): pl.pallas_call(functools.partial(branch_back_kernel, n, m), name='branch_...]
    reduce_scatter x8 -> x1, waiting for transfers between devices: 502 us -> 0.01 us  [local(): lax.psum_scatter(up_grad, 'dp', scatter_dimension=0, tiled=True)]
    all_gather x8 -> x3, waiting for transfers between devices: 454 us -> 0.06 us  [the longest x1 0.02 us: local(): out_w = lax.all_gather(out_line, 'dp', axis=1, tiled=True)]
    dot_general x24 -> x0, matrix products: 301 us -> none  [the longest x2 45.5 us: local(): jnp.einsum('hqk,qhd->khd', d_scores, query[start_row:stop_row], preferred...]
    unnamed x18 -> x4, waiting for transfers between devices: 33.9 us -> 0.07 us
    unnamed x125 -> x40, local copies, waits for them, and re-layouts: 35.6 us -> 5.01 us
    all_gather x1 -> x0, local copies, waits for them, and re-layouts: 23 us -> none  [local(): lax.all_gather(gate_up.astype(half_type), 'dp', axis=0, tiled=True)]
    convert_element_type x9 -> x2, other arithmetic: 21.6 us -> 3.16 us  [the longest x1 2.43 us: local(): in_low = jnp.transpose(in_weight, (1, 0, 2)).astype(BF)]
  transfers between devices with their start and end apart: 17 -> 4, of which waited for: 15 -> 0; matrix products, arithmetic and copies ran while one was open for 13% -> 2% of each run, Pallas kernels for 0% -> 62%
where the time goes in v1:
time: 641 us; the launch traced here: 637 us
  Pallas kernels  599 us (93%)
  other arithmetic  15.4 us (2%)
  between operations  14.3 us (2%)
  local copies, waits for them, and re-layouts  7.91 us (1%)
    pallas_call x1, Pallas kernels, branch_back(): pl.pallas_call(functools.partial(branch_back_kernel, n, m), name='branch_...  96.5 us
    pallas_call x1, Pallas kernels, input_back(): pl.pallas_call(functools.partial(input_back_kernel, n, m), name='input_ba...  93.9 us
    pallas_call x1, Pallas kernels, feed(): pl.pallas_call(functools.partial(feed_kernel, n), name='feed_forward', ou...  92.9 us
    pallas_call x1, Pallas kernels, gather_rows(): pl.pallas_call(functools.partial(rows_kernel, n), name='gather_tokens', o...  73.1 us
    pallas_call x1, Pallas kernels, project_branch(): pl.pallas_call(functools.partial(branch_kernel, n), name='branch', out_sh...  71.8 us
    pallas_call x1, Pallas kernels, attend(): pl.pallas_call(functools.partial(attend_kernel, n), name='attention_forwa...  71.4 us
    pallas_call x1, Pallas kernels, attend_back(): pl.pallas_call(functools.partial(attend_back_kernel, n), name='attention_...  65.9 us
    pallas_call x1, Pallas kernels, gather_first(): pl.pallas_call(functools.partial(first_kernel, n, m), name='gather_out_sh...  20.6 us
  transfers between devices with their start and end apart: 4, of which 0 were waited for; matrix products, arithmetic and copies ran while one was open for 2% of the time, Pallas kernels for 62%

profile of v1, /device:TPU:8, one launch (start us, length us, event | category | flops | bytes accessed | tf_op | source)
XLA Modules:
  0.0 636.7 jit_solution(11245524968205653569)
XLA Ops:
  7.3 2.4 convert_bitcast_fusion
  9.8 0.7 convert_element_type.11.out_ref
  10.5 0.6 pad.4.gain_ref
  11.1 20.6 %gather_out_shards.1 = (bf16[4,512,256]{2,1,0:T(8,128)(2,1)}, f32[8,8,256]{2,1,0:T(8,128)}) custom-call(bf16[512,256]{1,0:T(8,128)(2,1)} %convert_element_type.11.out_ref, f32[8,256]{1,0:T(8,128)} %pad.4.gain_ref), custom_call_target="tpu_custom_call" | custom-call | flops 20000000000 | bytes 40000000 | tf_op jit(solution)/shard_map/gather_out_shards/pallas_call | solution.py:471
  31.9 1.0 broadcast_in_dim.8.start_ref
  32.9 0.6 broadcast_in_dim.10.freq_ref
  33.5 73.1 %gather_tokens.1 = (bf16[4,256,2048]{2,1,0:T(8,128)(2,1)}, bf16[3,256,2048]{2,1,0:T(8,128)(2,1)}, f32[1024,128]{1,0:T(8,128)}, f32[1024,128]{1,0:T(8,128)}) custom-call(bf16[256,2048]{1,0:T(8,128)(2,1)} %x_ref.2, f32[256,2,2048]{2,1,0:T(2,128)} %w_ref.1, f32[2048,256]{1,0:T(8,128)} %down_hbm.1, s32[1024,128]{1,0:T(8,128)} %broadcast_in_dim.8.start_ref, ...), custom_call_target="tpu_custom_call" | custom-call | flops 65000001536 | bytes 130000000 | tf_op jit(solution)/shard_map/gather_tokens/pallas_call | solution.py:570
  106.7 71.4 %attention_forward.1 = (bf16[1024,2048]{1,0:T(8,128)(2,1)}, bf16[3,1024,512]{2,1,0:T(8,128)(2,1)}, bf16[1024,512]{1,0:T(8,128)(2,1)}, f32[8,1024]{1,0:T(8,128)},...) custom-call(bf16[1024,2048]{1,0:T(8,128)(2,1)} %bitcast.17, f32[8,2048]{1,0:T(8,128)} %bitcast.23, ...), custom_call_target="tpu_custom_call" | custom-call | flops 65000001536 | bytes 130000000 | tf_op jit(solution)/shard_map/attention_forward/pallas_call | solution.py:724
  178.1 71.8 %branch.1 = (bf16[1024,2048]{1,0:T(8,128)(2,1)}, f32[256,2048]{1,0:T(8,128)}) custom-call(bf16[1024,512]{1,0:T(8,128)(2,1)} %get-tuple-element.58.att_ref.att_hbm, bf16[2048,2048]{1,0:T(8,128)(2,1)} %all-gather.6.cloned.1.call-done.w_hbm, bf16[1024,2048]{1,0:T(8,128)(2,1)} %bitcast.18, f32[8,2048]{1,0:T(8,128)} %bitcast.24), custom_call_target="tpu_custom_call" | custom-call | flops 70000001024 | bytes 140000000 | tf_op jit(solution)/shard_map/branch/pallas_call | solution.py:819
  249.9 92.9 %feed_forward.1 = (bf16[1024,2048]{1,0:T(8,128)(2,1)}, bf16[2,1024,2048]{2,1,0:T(8,128)(2,1)}, f32[256,2048]{1,0:T(8,128)}) custom-call(bf16[1024,2048]{1,0:T(8,128)(2,1)} %get-tuple-element.60.h_hbm, bf16[1024,2048]{1,0:T(8,128)(2,1)} %bitcast.21, bf16[3,2048,2048]{2,1,0:T(8,128)(2,1)} %all-gather.8.cloned.1.call-done.w_hbm.feed_hbm), custom_call_target="tpu_custom_call" | custom-call | flops 95000002560 | bytes 190000000 | tf_op jit(solution)/shard_map/feed_forward/pallas_call | solution.py:964
  342.8 96.5 %branch_backward.1 = (f32[256,2048]{1,0:T(8,128)}, bf16[1024,512]{1,0:T(8,128)(2,1)}, f32[8,2048]{1,0:T(8,128)}, bf16[4,256,2048]{2,1,0:T(8,128)(2,1)}, bf16[16,...) custom-call(f32[256,2048]{1,0:T(8,128)} %get-tuple-element.63.d_two_ref, ...), custom_call_target="tpu_custom_call" | custom-call | flops 74999996416 | bytes 150000000 | tf_op jit(solution)/shard_map/branch_backward/pallas_call | solution.py:1194
  439.3 0.7 copy-done.14
  440.0 0.6 broadcast_in_dim.22.start_ref
  440.6 65.9 %attention_backward.1 = (bf16[3,1024,512]{2,1,0:T(8,128)(2,1)}, bf16[256,2048]{1,0:T(8,128)(2,1)}) custom-call(f32[8,1024]{1,0:T(8,128)} %get-tuple-element.56.lse_ref, s32[8,1024]{1,0:T(8,128)} %broadcast_in_dim.22.start_ref, bf16[3,1024,512]{2,1,0:T(8,128)(2,1)} %get-tuple-element.57.qkv_hbm, bf16[1024,512]{1,0:T(8,128)(2,1)} %get-tuple-element.67.d_att_hbm, ...), custom_call_target="tpu_custom_call" | custom-call | flops 80000000000 | bytes 160000000 | tf_op jit(solution)/shard_map/attention_backward/pallas_call | solution.py:1381
  506.6 93.9 %input_backward.1 = (f32[256,2048]{1,0:T(8,128)}, f32[3,256,512]{2,1,0:T(8,128)}, f32[512,256]{1,0:T(8,128)}, f32[8,256]{1,0:T(8,128)}) custom-call(bf16[3,1024,512]{2,1,0:T(8,128)(2,1)} %get-tuple-element.70.d_ref, bf16[3,2048,512]{2,1,0:T(8,128)(2,1)} %all-gather.4.cloned.1.call-done.w_hbm.w_ref, bf16[256,2048]{1,0:T(8,128)(2,1)} %x_ref.2, ...), custom_call_target="tpu_custom_call" | custom-call | flops 74999996416 | bytes 150000000 | tf_op jit(solution)/shard_map/input_backward/pallas_call | solution.py:1613
  600.5 1.5 multiply_subtract_fusion.3
  602.0 2.4 multiply_subtract_fusion.2
  604.5 4.6 multiply_subtract_fusion.1
  609.1 1.0 copy-done.4
  610.1 3.7 multiply_subtract_fusion
  613.8 12.9 %adam_gate_up.1 = (f32[256,2,2048]{2,1,0:T(2,128)}, f32[256,2,2048]{2,1,0:T(2,128)}, f32[256,2,2048]{2,1,0:T(2,128)}) custom-call(f32[256,2,2048]{2,1,0:T(2,128)} %w_ref.1, f32[256,2,2048]{2,1,0:T(2,128)} %first_ref.1, f32[256,2,2048]{2,1,0:T(2,128)} %second_ref.1, bf16[2,256,2048]{2,1,0:T(8,128)(2,1)} %reduce-scatter.2.cloned.1.call-done.grad_ref), custom_call_target="tpu_custom_call" | custom-call | flops 10000000000 | bytes 20000000 | tf_op jit(solution)/shard_map/adam_gate_up/pallas_call | solution.py:1681
  626.7 1.0 copy.37
  627.7 1.0 copy-done.7
  628.7 1.3 copy.38
  (51 shorter events, 0.5 us)
Async XLA Ops:
  7.2 2.6 copy-start.5
  7.2 3.3 copy-start.15
  7.2 99.5 %all-gather.4.cloned.1.call-start = ((), (), s32[]{:S(2)}) async-start(), calls=%async_computation.1 | async-start | bytes 7077888 | tf_op jit(solution)/shard_map/all_gather | solution.py:1738
  9.7 168.4 %all-gather.6.cloned.1.call-start = ((), (), s32[]{:S(2)}) async-start(), calls=%async_computation.2 | async-start | bytes 9437184 | tf_op jit(solution)/shard_map/all_gather | solution.py:1742
  11.1 20.8 %copy-start.13 = (s32[1024]{0:T(1024)S(1)}, s32[1024]{0:T(1024)}, u32[]{:S(2)}) copy-start(s32[1024]{0:T(1024)} %param.20) | copy-start | bytes 12292
  31.7 218.2 %all-gather.8.cloned.1.call-start = ((), (), s32[]{:S(2)}) async-start(), calls=%async_computation.3 | async-start | bytes 28311552 | tf_op jit(solution)/shard_map/all_gather | solution.py:1747
  106.6 507.2 %reduce-scatter.2.cloned.1.call-start = ((), (), s32[]{:S(2)}) async-start(), calls=%async_computation.4 | async-start | bytes 18874368 | tf_op jit(solution)/shard_map/reduce_scatter | solution.py:1770
  439.3 0.7 copy-start.14
  506.5 94.0 %copy-start.16 = (f32[2,256]{1,0:T(2,128)S(1)}, f32[2,256]{1,0:T(2,128)}, u32[]{:S(2)}) copy-start(f32[2,256]{1,0:T(2,128)} %param.33) | copy-start | bytes 6148
  506.5 94.0 %copy-start.17 = (f32[2,256]{1,0:T(2,128)S(1)}, f32[2,256]{1,0:T(2,128)}, u32[]{:S(2)}) copy-start(f32[2,256]{1,0:T(2,128)} %param.35) | copy-start | bytes 6148
  506.6 94.0 %copy-start.18 = (f32[2,256]{1,0:T(2,128)S(1)}, f32[2,256]{1,0:T(2,128)}, u32[]{:S(2)}) copy-start(f32[2,256]{1,0:T(2,128)} %param.34) | copy-start | bytes 6148
  506.6 95.4 %copy-start.6 = (f32[512,256]{1,0:T(8,128)S(1)}, f32[512,256]{1,0:T(8,128)}, u32[]{:S(2)}) copy-start(f32[512,256]{1,0:T(8,128)} %param.24) | copy-start | bytes 1572868
  506.6 95.4 %copy-start.11 = (f32[512,256]{1,0:T(8,128)S(1)}, f32[512,256]{1,0:T(8,128)}, u32[]{:S(2)}) copy-start(f32[512,256]{1,0:T(8,128)} %param.26) | copy-start | bytes 1572868
  506.6 95.4 %copy-start.12 = (f32[512,256]{1,0:T(8,128)S(1)}, f32[512,256]{1,0:T(8,128)}, u32[]{:S(2)}) copy-start(f32[512,256]{1,0:T(8,128)} %param.25) | copy-start | bytes 1572868
  506.6 97.8 %copy-start.9 = (f32[256,3,512]{2,0,1:T(8,128)S(1)}, f32[256,3,512]{2,0,1:T(8,128)}, u32[]{:S(2)}) copy-start(f32[256,3,512]{2,0,1:T(8,128)} %param.22) | copy-start | bytes 4718596
  600.5 3.9 copy-start
  600.5 3.9 copy-start.8
  604.4 4.7 copy-start.1
  604.5 4.7 copy-start.2
  604.5 4.7 copy-start.3
  604.5 5.6 copy-start.4
  613.8 13.0 %copy-start.10 = (bf16[256,2048]{1,0:T(8,128)(2,1)S(1)}, bf16[256,2048]{1,0:T(8,128)(2,1)}, u32[]{:S(2)}) copy-start(bf16[256,2048]{1,0:T(8,128)(2,1)} %get-tuple-element.114) | copy-start | bytes 3145732
  626.7 2.0 copy-start.7
Sparse Core Ops, SparseCore 0:
  10.5 46.6 all-gather.3
  59.1 55.9 all-gather.5
  117.0 125.3 all-gather.7
  439.4 132.6 reduce-scatter.1

commit v2 on v1

--- a/solution.py
+++ b/solution.py
@@ -279,7 +279,8 @@
 
 
 class ChipScatter:
-    def __init__(self, line, m, mine, theirs, half, box, pair_send, pair_recv, chip_send, chip_recv):
+    def __init__(self, line, m, early, mine, theirs, half, box, pair_send, pair_recv, chip_send, chip_recv):
+        self.early = early
         self.chips = m // 2
         self.square = self.chips == 4
         self.chip, self.core = line // 2, lax.rem(line, 2)
@@ -340,8 +341,8 @@
         hop, other = self.steps[at]
         if other:
             self.to_pair(hop).start()
-            if at >= 2:
-                self.combine(self.steps[at - 1][0])
+        if at >= 2 and other == self.early:
+            self.combine(self.steps[at - 1 if self.early else at - 2][0])
 
     def combine(self, hop):
         self.to_pair(hop).wait_recv()
@@ -1030,7 +1031,7 @@
 ):
     me = lax.axis_index("tensor")
     line = lax.axis_index("dp")
-    down_sum = ChipScatter(line, m, *chip_scratch)
+    down_sum = ChipScatter(line, m, False, *chip_scratch)
     rows_each, depth = hidden_ref.shape
     width = d_att_ref.shape[1]
     size = rows_each // CHUNKS
@@ -1172,11 +1173,11 @@
     arrived(2)
     lax.fori_loop(m // 2, m, up_piece, 0)
     scatter.relays(0, scatter.events)
-    down_sum.arrive()
-    down_ref[...] = jnp.transpose(down_sum.result(0))
     for step in range(3, n):
         gather.advance(step)
         arrived(step)
+    down_sum.arrive()
+    down_ref[...] = jnp.transpose(down_sum.result(0))
     for kind in range(2):
         out_copy(m - 1, kind).wait()
     for shard in range(n):
@@ -1462,7 +1463,7 @@
     line = lax.axis_index("dp")
     rows_each, depth = x_ref.shape
     kinds = in_ref.shape[0] + 1
-    mixed_sum = ChipScatter(line, m, *chip_scratch)
+    mixed_sum = ChipScatter(line, m, True, *chip_scratch)
     each = in_ref.shape[1]
     fetch_att = pltpu.make_async_copy(att_hbm, att, att_sem)
     fetch_x = pltpu.make_async_copy(all_x_hbm, all_x, x_sem)
@@ -1547,14 +1548,15 @@
         if 4 * (at + 1) // m - 1 > served:
             scatter.relay(served)
             served += 1
+        if at == m // 2 - 1:
+            for i in range(2, n - 1):
+                term(i)
+    mixed_sum.forward()
     mixed_sum.combine(0)
-    for i in range(2, n):
-        term(i)
+    term(n - 1)
     for hop in range(1, n):
         across(hop).start()
-    scatter.relays(served, served + 1)
-    mixed_sum.forward()
-    scatter.relays(served + 1, served + 3)
+    scatter.relays(served, served + 3)
     for hop in range(1, n):
         across(hop).wait_recv()
     gain_total = gain_part[...]

time: 641 us -> 634 us (0.989); the launches traced: 637 us -> 623 us
  Pallas kernels: 599 us -> 585 us
    pallas_call x1, Pallas kernels: 96.5 us -> 86.3 us  [branch_back(): pl.pallas_call(functools.partial(branch_back_kernel, n, m), name='branch_...]
  transfers between devices with their start and end apart: 4 -> 4, of which waited for: 0 -> 0; matrix products, arithmetic and copies ran while one was open for 2% -> 3% of each run, Pallas kernels for 62% -> 63%
where the time goes in v2:
time: 634 us; the launch traced here: 623 us
  Pallas kernels  585 us (92%)
  other arithmetic  15.4 us (2%)
  between operations  14.3 us (2%)
  local copies, waits for them, and re-layouts  7.91 us (1%)
    pallas_call x1, Pallas kernels, feed(): pl.pallas_call(functools.partial(feed_kernel, n), name='feed_forward', ou...  92.9 us
    pallas_call x1, Pallas kernels, input_back(): pl.pallas_call(functools.partial(input_back_kernel, n, m), name='input_ba...  91.7 us
    pallas_call x1, Pallas kernels, branch_back(): pl.pallas_call(functools.partial(branch_back_kernel, n, m), name='branch_...  86.3 us
    pallas_call x1, Pallas kernels, gather_rows(): pl.pallas_call(functools.partial(rows_kernel, n), name='gather_tokens', o...  73.1 us
    pallas_call x1, Pallas kernels, project_branch(): pl.pallas_call(functools.partial(branch_kernel, n), name='branch', out_sh...  71.8 us
    pallas_call x1, Pallas kernels, attend(): pl.pallas_call(functools.partial(attend_kernel, n), name='attention_forwa...  71.4 us
    pallas_call x1, Pallas kernels, attend_back(): pl.pallas_call(functools.partial(attend_back_kernel, n), name='attention_...  64.5 us
    pallas_call x1, Pallas kernels, gather_first(): pl.pallas_call(functools.partial(first_kernel, n, m), name='gather_out_sh...  20.6 us
  transfers between devices with their start and end apart: 4, of which 0 were waited for; matrix products, arithmetic and copies ran while one was open for 3% of the time, Pallas kernels for 63%

profile of v2, /device:TPU:8, one launch (start us, length us, event | category | flops | bytes accessed | tf_op | source)
XLA Modules:
  0.0 623.1 jit_solution(14147868450298704151)
XLA Ops:
  7.3 2.4 convert_bitcast_fusion
  9.8 0.7 convert_element_type.11.out_ref
  10.5 0.6 pad.4.gain_ref
  11.1 20.6 %gather_out_shards.1 = (bf16[4,512,256]{2,1,0:T(8,128)(2,1)}, f32[8,8,256]{2,1,0:T(8,128)}) custom-call(bf16[512,256]{1,0:T(8,128)(2,1)} %convert_element_type.11.out_ref, f32[8,256]{1,0:T(8,128)} %pad.4.gain_ref), custom_call_target="tpu_custom_call" | custom-call | flops 20000000000 | bytes 40000000 | tf_op jit(solution)/shard_map/gather_out_shards/pallas_call | solution.py:472
  31.9 1.0 broadcast_in_dim.8.start_ref
  32.9 0.6 broadcast_in_dim.10.freq_ref
  33.5 73.1 %gather_tokens.1 = (bf16[4,256,2048]{2,1,0:T(8,128)(2,1)}, bf16[3,256,2048]{2,1,0:T(8,128)(2,1)}, f32[1024,128]{1,0:T(8,128)}, f32[1024,128]{1,0:T(8,128)}) custom-call(bf16[256,2048]{1,0:T(8,128)(2,1)} %x_ref.2, f32[256,2,2048]{2,1,0:T(2,128)} %w_ref.1, f32[2048,256]{1,0:T(8,128)} %down_hbm.1, s32[1024,128]{1,0:T(8,128)} %broadcast_in_dim.8.start_ref, ...), custom_call_target="tpu_custom_call" | custom-call | flops 65000001536 | bytes 130000000 | tf_op jit(solution)/shard_map/gather_tokens/pallas_call | solution.py:571
  106.7 71.4 %attention_forward.1 = (bf16[1024,2048]{1,0:T(8,128)(2,1)}, bf16[3,1024,512]{2,1,0:T(8,128)(2,1)}, bf16[1024,512]{1,0:T(8,128)(2,1)}, f32[8,1024]{1,0:T(8,128)},...) custom-call(bf16[1024,2048]{1,0:T(8,128)(2,1)} %bitcast.17, f32[8,2048]{1,0:T(8,128)} %bitcast.23, ...), custom_call_target="tpu_custom_call" | custom-call | flops 65000001536 | bytes 130000000 | tf_op jit(solution)/shard_map/attention_forward/pallas_call | solution.py:725
  178.1 71.8 %branch.1 = (bf16[1024,2048]{1,0:T(8,128)(2,1)}, f32[256,2048]{1,0:T(8,128)}) custom-call(bf16[1024,512]{1,0:T(8,128)(2,1)} %get-tuple-element.58.att_ref.att_hbm, bf16[2048,2048]{1,0:T(8,128)(2,1)} %all-gather.6.cloned.1.call-done.w_hbm, bf16[1024,2048]{1,0:T(8,128)(2,1)} %bitcast.18, f32[8,2048]{1,0:T(8,128)} %bitcast.24), custom_call_target="tpu_custom_call" | custom-call | flops 70000001024 | bytes 140000000 | tf_op jit(solution)/shard_map/branch/pallas_call | solution.py:820
  249.9 92.9 %feed_forward.1 = (bf16[1024,2048]{1,0:T(8,128)(2,1)}, bf16[2,1024,2048]{2,1,0:T(8,128)(2,1)}, f32[256,2048]{1,0:T(8,128)}) custom-call(bf16[1024,2048]{1,0:T(8,128)(2,1)} %get-tuple-element.60.h_hbm, bf16[1024,2048]{1,0:T(8,128)(2,1)} %bitcast.21, bf16[3,2048,2048]{2,1,0:T(8,128)(2,1)} %all-gather.8.cloned.1.call-done.w_hbm.feed_hbm), custom_call_target="tpu_custom_call" | custom-call | flops 95000002560 | bytes 190000000 | tf_op jit(solution)/shard_map/feed_forward/pallas_call | solution.py:965
  342.8 86.3 %branch_backward.1 = (f32[256,2048]{1,0:T(8,128)}, bf16[1024,512]{1,0:T(8,128)(2,1)}, f32[8,2048]{1,0:T(8,128)}, bf16[4,256,2048]{2,1,0:T(8,128)(2,1)}, bf16[16,...) custom-call(f32[256,2048]{1,0:T(8,128)} %get-tuple-element.63.d_two_ref, ...), custom_call_target="tpu_custom_call" | custom-call | flops 74999996416 | bytes 150000000 | tf_op jit(solution)/shard_map/branch_backward/pallas_call | solution.py:1195
  429.2 0.7 copy-done.14
  429.8 0.6 broadcast_in_dim.22.start_ref
  430.4 64.5 %attention_backward.1 = (bf16[3,1024,512]{2,1,0:T(8,128)(2,1)}, bf16[256,2048]{1,0:T(8,128)(2,1)}) custom-call(f32[8,1024]{1,0:T(8,128)} %get-tuple-element.56.lse_ref, s32[8,1024]{1,0:T(8,128)} %broadcast_in_dim.22.start_ref, bf16[3,1024,512]{2,1,0:T(8,128)(2,1)} %get-tuple-element.57.qkv_hbm, bf16[1024,512]{1,0:T(8,128)(2,1)} %get-tuple-element.67.d_att_hbm, ...), custom_call_target="tpu_custom_call" | custom-call | flops 80000000000 | bytes 160000000 | tf_op jit(solution)/shard_map/attention_backward/pallas_call | solution.py:1382
  495.1 91.7 %input_backward.1 = (f32[256,2048]{1,0:T(8,128)}, f32[3,256,512]{2,1,0:T(8,128)}, f32[512,256]{1,0:T(8,128)}, f32[8,256]{1,0:T(8,128)}) custom-call(bf16[3,1024,512]{2,1,0:T(8,128)(2,1)} %get-tuple-element.70.d_ref, bf16[3,2048,512]{2,1,0:T(8,128)(2,1)} %all-gather.4.cloned.1.call-done.w_hbm.w_ref, bf16[256,2048]{1,0:T(8,128)(2,1)} %x_ref.2, ...), custom_call_target="tpu_custom_call" | custom-call | flops 74999996416 | bytes 150000000 | tf_op jit(solution)/shard_map/input_backward/pallas_call | solution.py:1615
  586.9 1.5 multiply_subtract_fusion.3
  588.3 2.4 multiply_subtract_fusion.2
  590.8 4.6 multiply_subtract_fusion.1
  595.4 1.0 copy-done.4
  596.4 3.7 multiply_subtract_fusion
  600.1 12.9 %adam_gate_up.1 = (f32[256,2,2048]{2,1,0:T(2,128)}, f32[256,2,2048]{2,1,0:T(2,128)}, f32[256,2,2048]{2,1,0:T(2,128)}) custom-call(f32[256,2,2048]{2,1,0:T(2,128)} %w_ref.1, f32[256,2,2048]{2,1,0:T(2,128)} %first_ref.1, f32[256,2,2048]{2,1,0:T(2,128)} %second_ref.1, bf16[2,256,2048]{2,1,0:T(8,128)(2,1)} %reduce-scatter.2.cloned.1.call-done.grad_ref), custom_call_target="tpu_custom_call" | custom-call | flops 10000000000 | bytes 20000000 | tf_op jit(solution)/shard_map/adam_gate_up/pallas_call | solution.py:1683
  613.1 1.0 copy.37
  614.0 1.0 copy-done.7
  615.0 1.3 copy.38
  (51 shorter events, 0.5 us)
Async XLA Ops:
  7.2 2.6 copy-start.5
  7.2 3.3 copy-start.15
  7.2 99.5 %all-gather.4.cloned.1.call-start = ((), (), s32[]{:S(2)}) async-start(), calls=%async_computation.1 | async-start | bytes 7077888 | tf_op jit(solution)/shard_map/all_gather | solution.py:1740
  9.7 168.4 %all-gather.6.cloned.1.call-start = ((), (), s32[]{:S(2)}) async-start(), calls=%async_computation.2 | async-start | bytes 9437184 | tf_op jit(solution)/shard_map/all_gather | solution.py:1744
  11.1 20.8 %copy-start.13 = (s32[1024]{0:T(1024)S(1)}, s32[1024]{0:T(1024)}, u32[]{:S(2)}) copy-start(s32[1024]{0:T(1024)} %param.20) | copy-start | bytes 12292
  31.7 218.2 %all-gather.8.cloned.1.call-start = ((), (), s32[]{:S(2)}) async-start(), calls=%async_computation.3 | async-start | bytes 28311552 | tf_op jit(solution)/shard_map/all_gather | solution.py:1749
  106.6 493.5 %reduce-scatter.2.cloned.1.call-start = ((), (), s32[]{:S(2)}) async-start(), calls=%async_computation.4 | async-start | bytes 18874368 | tf_op jit(solution)/shard_map/reduce_scatter | solution.py:1772
  429.1 0.7 copy-start.14
  495.0 91.9 %copy-start.16 = (f32[2,256]{1,0:T(2,128)S(1)}, f32[2,256]{1,0:T(2,128)}, u32[]{:S(2)}) copy-start(f32[2,256]{1,0:T(2,128)} %param.33) | copy-start | bytes 6148
  495.0 91.9 %copy-start.17 = (f32[2,256]{1,0:T(2,128)S(1)}, f32[2,256]{1,0:T(2,128)}, u32[]{:S(2)}) copy-start(f32[2,256]{1,0:T(2,128)} %param.35) | copy-start | bytes 6148
  495.0 91.9 %copy-start.18 = (f32[2,256]{1,0:T(2,128)S(1)}, f32[2,256]{1,0:T(2,128)}, u32[]{:S(2)}) copy-start(f32[2,256]{1,0:T(2,128)} %param.34) | copy-start | bytes 6148
  495.0 93.3 %copy-start.6 = (f32[512,256]{1,0:T(8,128)S(1)}, f32[512,256]{1,0:T(8,128)}, u32[]{:S(2)}) copy-start(f32[512,256]{1,0:T(8,128)} %param.24) | copy-start | bytes 1572868
  495.0 93.3 %copy-start.11 = (f32[512,256]{1,0:T(8,128)S(1)}, f32[512,256]{1,0:T(8,128)}, u32[]{:S(2)}) copy-start(f32[512,256]{1,0:T(8,128)} %param.26) | copy-start | bytes 1572868
  495.0 93.3 %copy-start.12 = (f32[512,256]{1,0:T(8,128)S(1)}, f32[512,256]{1,0:T(8,128)}, u32[]{:S(2)}) copy-start(f32[512,256]{1,0:T(8,128)} %param.25) | copy-start | bytes 1572868
  495.1 95.7 %copy-start.9 = (f32[256,3,512]{2,0,1:T(8,128)S(1)}, f32[256,3,512]{2,0,1:T(8,128)}, u32[]{:S(2)}) copy-start(f32[256,3,512]{2,0,1:T(8,128)} %param.22) | copy-start | bytes 4718596
  586.8 3.9 copy-start
  586.8 3.9 copy-start.8
  590.8 4.7 copy-start.1
  590.8 4.7 copy-start.2
  590.8 4.7 copy-start.3
  590.8 5.6 copy-start.4
  600.1 13.0 %copy-start.10 = (bf16[256,2048]{1,0:T(8,128)(2,1)S(1)}, bf16[256,2048]{1,0:T(8,128)(2,1)}, u32[]{:S(2)}) copy-start(bf16[256,2048]{1,0:T(8,128)(2,1)} %get-tuple-element.114) | copy-start | bytes 3145732
  613.1 2.0 copy-start.7
Sparse Core Ops, SparseCore 0:
  10.5 46.6 all-gather.3
  59.1 55.9 all-gather.5
  117.0 125.3 all-gather.7
  429.3 138.0 reduce-scatter.1
